TPU v7x, 32 devices: a whole 2x2x4 slice. The times are simulated.
32 devices in a mesh: group: 16 (over z, y, x), kv: 2 (over core).
Axes of the slice: x: 2, y: 2, z: 4, core: 2. Of those that a mesh axis runs over, the one named last changes fastest.
Arguments:
- lengths: int32 [16], P('group'), may hold values from 2048 to 8192, as said below
- latents: bfloat16 [16, 8192, 160], P('group', 'kv'), may hold values from -6 to 6
- codes: bfloat16 [16, 8192, 1024], P('group', 'kv'), may hold values from -10 to 10
- scales: bfloat16 [16, 32, 8], P('group', 'kv'), may hold values from 0.5 to 4
- queries: bfloat16 [16, 8, 8192], P('group'), may hold values from -900 to 900
- new_keys: bfloat16 [16, 8, 1024], P('group'), may hold values from -8 to 8
- new_values: bfloat16 [16, 8, 1024], P('group'), may hold values from -12 to 12
- key_factor: bfloat16 [160, 1024], replicated, may hold values from -0.5 to 0.5
- out_weight: bfloat16 [8192, 8192], P('kv', 'group'), may hold values from -0.0625 to 0.0625
Outputs:
- layer_out: float32 [128, 8192], P('kv', 'group')
Inputs may be any that keep to these rules, and one draw needn't show every extreme that they name: `lengths`: one request has exactly 8192 cached tokens and one exactly 2048.
All inputs are finite; a program needn't handle non-finite values.
Results may differ from a plain program's by a relative error of at most 0.0087.
Values may be sent and summed in bfloat16 or wider, within the bound.
A program may use at most 128 MiB of HBM per device.

v0:
```python
import jax
import jax.numpy as jnp
from jax import lax
from jax.sharding import PartitionSpec as P

HEADS = 64
KV_HEADS = 8
HEAD_DIM = 128
BLK = 256
CTX_DEV = 4096
Q_TOK = 8


ROPE_BASE = 500000.0
NEG_FILL = -1e30


def merged(shard, axis, combine):
    everything = jax.tree.map(lambda part: lax.all_gather(part, axis), shard)
    initial = jax.tree.map(lambda part: part[0], everything)

    def lap(k, so_far):
        return combine(so_far, jax.tree.map(lambda part: part[k], everything))

    return lax.fori_loop(1, lax.axis_size(axis), lap, initial)


def rotate(key_before_rotary, positions):
    half_dim = HEAD_DIM // 2
    frequency = ROPE_BASE ** (-(jnp.arange(half_dim, dtype=jnp.float32) * 2.0) / HEAD_DIM)
    angles = positions.astype(jnp.float32)[:, None] * frequency[None, :]
    cosine = jnp.cos(angles)[:, None, :]
    sine_val = jnp.sin(angles)[:, None, :]
    lower_half = key_before_rotary[..., :half_dim]
    upper_half = key_before_rotary[..., half_dim:]
    return jnp.concatenate(
        [lower_half * cosine - upper_half * sine_val, upper_half * cosine + lower_half * sine_val],
        axis=-1,
    )


def attend_block(
    carried, latent, code_rows, scale_row, query_matrix_rows, key_factor, start_pos, length
):
    peak_score, totals, numerator = carried
    key_before_rotary = jnp.dot(latent, key_factor, preferred_element_type=jnp.float32).reshape(
        BLK, KV_HEADS, HEAD_DIM
    )
    positions = start_pos + jnp.arange(BLK, dtype=jnp.int32)
    rotary_applied = rotate(key_before_rotary, positions).astype(jnp.bfloat16)
    scores = jnp.einsum(
        "onvs,xns->onvx", query_matrix_rows, rotary_applied, preferred_element_type=jnp.float32
    ) * HEAD_DIM ** (-0.5)
    valid_mask = (positions < length)[None, None, None, :]
    scores = jnp.where(valid_mask, scores, NEG_FILL)
    new_peak = jnp.maximum(peak_score, jnp.max(scores, axis=-1))
    shrink_by = jnp.exp(peak_score - new_peak)
    weights = jnp.where(valid_mask, jnp.exp(scores - new_peak[..., None]), 0.0)
    totals = totals * shrink_by + jnp.sum(weights, axis=-1)
    value_rows = code_rows.reshape(BLK, KV_HEADS, HEAD_DIM)
    block_part = jnp.einsum(
        "lahy,yaw->lahw",
        weights.astype(jnp.bfloat16),
        value_rows,
        preferred_element_type=jnp.float32,
    )
    numerator = (
        numerator * shrink_by[..., None]
        + block_part * scale_row.astype(jnp.float32)[None, :, None, None]
    )
    return (new_peak, totals, numerator)


def run_blocks(
    carried,
    latent,
    code_rows,
    scale_rows,
    query_matrix_rows,
    key_factor,
    block_count,
    base_pos,
    length,
):

    def advance(block_index, state_now):
        lat_block = lax.dynamic_slice_in_dim(latent, block_index * BLK, BLK, 0)
        code_block = lax.dynamic_slice_in_dim(code_rows, block_index * BLK, BLK, 0)
        scale_block = lax.dynamic_index_in_dim(scale_rows, block_index, 0, keepdims=False)
        return attend_block(
            state_now,
            lat_block,
            code_block,
            scale_block,
            query_matrix_rows,
            key_factor,
            base_pos + block_index * BLK,
            length,
        )

    return lax.fori_loop(0, block_count, advance, carried)


def live_blocks(length, owner_index):
    filled = jnp.clip(length - owner_index * CTX_DEV, 0, CTX_DEV)
    return (filled + BLK - 1) // BLK


def combine_triples(first_triple, second_triple):
    peak_a, total_a, numer_a = first_triple
    peak_b, total_b, numer_b = second_triple
    joint_peak = jnp.maximum(peak_a, peak_b)
    weight_a = jnp.exp(peak_a - joint_peak)
    weight_b = jnp.exp(peak_b - joint_peak)
    return (
        joint_peak,
        total_a * weight_a + total_b * weight_b,
        numer_a * weight_a[..., None] + numer_b * weight_b[..., None],
    )


def body(lengths, latents, codes, scales, queries, new_keys, new_values, key_factor, out_weight):
    kv_count = lax.axis_size("kv")
    kv_at = lax.axis_index("kv")
    groups = HEADS // KV_HEADS
    requests = latents.shape[0]
    heads_dev = HEADS // kv_count
    query_full_set = queries.reshape(requests, Q_TOK, KV_HEADS, groups, HEAD_DIM)
    order_mask = jnp.arange(Q_TOK)[None, :] <= jnp.arange(Q_TOK)[:, None]
    causal = jnp.logical_and(order_mask[:, None, None, :], kv_at == 0)
    query_matrix_rows = query_full_set[0]
    fresh_keys = new_keys[0].reshape(Q_TOK, KV_HEADS, HEAD_DIM)
    fresh_vals = new_values[0].reshape(Q_TOK, KV_HEADS, HEAD_DIM)
    fresh_scores = jnp.einsum(
        "tkgd,ukd->tkgu", query_matrix_rows, fresh_keys, preferred_element_type=jnp.float32
    ) * HEAD_DIM ** (-0.5)
    fresh_scores = jnp.where(causal, fresh_scores, NEG_FILL)
    start_peak = jnp.max(fresh_scores, axis=-1)
    fresh_weights = jnp.where(causal, jnp.exp(fresh_scores - start_peak[..., None]), 0.0)
    start_total = jnp.sum(fresh_weights, axis=-1)
    start_numer = jnp.einsum(
        "tkgu,ukd->tkgd",
        fresh_weights.astype(jnp.bfloat16),
        fresh_vals,
        preferred_element_type=jnp.float32,
    )
    state_now = (start_peak, start_total, start_numer)
    length = lengths[0]
    own_count = live_blocks(length, kv_at)
    state_now = run_blocks(
        state_now,
        latents[0],
        codes[0],
        scales[0],
        query_matrix_rows,
        key_factor,
        own_count,
        kv_at * CTX_DEV,
        length,
    )
    states = [state_now]
    peaks = jnp.stack([triple[0] for triple in states])
    totals = jnp.stack([triple[1] for triple in states])
    numerator = jnp.stack([triple[2] for triple in states])
    merged_peak, merged_total, merged_numer = merged(
        (peaks, totals, numerator), "kv", combine_triples
    )
    merged_total = merged_total.reshape(requests, Q_TOK, HEADS)
    merged_numer = merged_numer.reshape(requests, Q_TOK, HEADS, HEAD_DIM)
    totals_dev = lax.dynamic_slice_in_dim(merged_total, kv_at * heads_dev, heads_dev, 2)
    numer_dev = lax.dynamic_slice_in_dim(merged_numer, kv_at * heads_dev, heads_dev, 2)
    attended = (
        (numer_dev / totals_dev[..., None])
        .astype(jnp.bfloat16)
        .reshape(requests * Q_TOK, heads_dev * HEAD_DIM)
    )
    all_rows = lax.all_gather(attended, "group", axis=0, tiled=True)
    return lax.psum_scatter(
        jnp.dot(all_rows, out_weight, preferred_element_type=jnp.float32),
        "kv",
        scatter_dimension=0,
        tiled=True,
    )


def solution(mesh):
    placed = (
        P("group"),
        P("group", "kv", None),
        P("group", "kv", None),
        P("group", "kv", None),
        P("group", None, None),
        P("group", None, None),
        P("group", None, None),
        P(),
        P("kv", "group"),
    )
    return jax.shard_map(
        body, mesh=mesh, in_specs=placed, out_specs=P("kv", "group"), check_vma=False
    )
```

profile of v0, /device:TPU:0, one launch (start us, length us, event | category | flops | bytes accessed | tf_op | source)
XLA Modules:
  0.0 199.0 jit_solution(18238814645791615959)
XLA Ops:
  8.2 1.6 fusion.48
  10.3 11.3 %copy.37 = bf16[1,4096,1024]{1,2,0:T(8,128)(2,1)} copy(bf16[1,4096,1024]{2,1,0:T(8,128)(2,1)} %param.13) | data formatting | bytes 16777216 | tf_op args[2]
  21.7 2.4 %copy.36 = bf16[1,4096,160]{2,1,0:T(8,128)(2,1)} copy(bf16[1,4096,160]{1,2,0:T(8,128)(2,1)S(1)} %copy-done.2) | data formatting | bytes 2621440 | tf_op args[1]
  24.2 91.7 %while.2 = (s32[]{:T(128)}, f32[8,8,8]{2,0,1:T(8,128)S(1)}, f32[8,8,8]{2,0,1:T(8,128)S(1)}, f32[8,8,8,128]{3,2,0,1:T(8,128)S(1)}, s32[]{:T(128)}, /*index=5*/s32...) while((s32[]{:T(128)}, f32[8,8,8]{2,0,1:T(8,128)S(1)}, ...), condition=%wide.region_5.6_spmd, body=%wide.region_2.5_spmd.sunk | while | flops 154486992 | bytes 11898721 | solution.py:101
  24.2 1.2 convolution_bitcast_fusion.3
  28.4 1.1 constant_dynamic-slice_fusion.5
  29.9 1.2 convolution_bitcast_fusion.3
  34.1 1.1 constant_dynamic-slice_fusion.5
  35.7 1.2 convolution_bitcast_fusion.3
  39.9 1.1 constant_dynamic-slice_fusion.5
  41.4 1.2 convolution_bitcast_fusion.3
  45.6 1.1 constant_dynamic-slice_fusion.5
  47.1 1.2 convolution_bitcast_fusion.3
  52.9 1.2 convolution_bitcast_fusion.3
  58.6 1.2 convolution_bitcast_fusion.3
  64.3 1.2 convolution_bitcast_fusion.3
  68.6 1.1 constant_dynamic-slice_fusion.5
  70.1 1.2 convolution_bitcast_fusion.3
  75.8 1.2 convolution_bitcast_fusion.3
  81.5 1.2 convolution_bitcast_fusion.3
  87.3 1.2 convolution_bitcast_fusion.3
  93.0 1.2 convolution_bitcast_fusion.3
  98.7 1.2 convolution_bitcast_fusion.3
  103.0 1.1 constant_dynamic-slice_fusion.5
  104.5 1.2 convolution_bitcast_fusion.3
  110.2 1.2 convolution_bitcast_fusion.3
  115.9 1.9 all-gather.1
  118.1 2.2 %all-gather = f32[16,8,8,128]{3,2,1,0:T(8,128)S(1)} all-gather(f32[8,8,8,128]{3,2,1,0:T(8,128)S(1)} %copy.40), channel_id=2, replica_groups=mesh['group'=16,'kv'=2] {'kv'}, dimensions={0}, use_global_device_ids=true | all-gather | bytes 786432 | tf_op jit(solution)/shard_map/all_gather | solution.py:19
  120.4 1.9 all-gather.2
  123.5 58.1 %all-gather.5.cloned.1.call-done = bf16[128,4096]{1,0:T(8,128)(2,1)} async-done(((bf16[8,4096]{1,0:T(8,128)(2,1)}), bf16[128,4096]{1,0:T(8,128)(2,1)}) %all-gather.5.cloned.1.call-update) | async-done | bytes 1048592 | tf_op jit(solution)/shard_map/all_gather | solution.py:177
  181.6 3.9 %fusion.49 = f32[128,512]{1,0:T(8,128)} fusion(bf16[128,4096]{1,0:T(8,128)(2,1)} %all-gather.5.cloned.1.call-done, bf16[4096,512]{1,0:T(8,128)(2,1)} %param.19), kind=kOutput, calls=%fused_computation.79 | convolution fusion | flops 536870912 | bytes 5505024 | tf_op jit(solution)/shard_map/dot_general | solution.py:179
  185.5 6.6 %reduce-scatter.2.cloned.1.call-done = f32[64,512]{1,0:T(8,128)} async-done(((f32[128,512]{1,0:T(8,128)}), f32[64,512]{1,0:T(8,128)}) %reduce-scatter.2.cloned.1.call-update) | async-done | bytes 131088 | tf_op jit(solution)/shard_map/reduce_scatter | solution.py:178
  (272 shorter events, 67.2 us)
Async XLA Ops:
  6.5 3.4 %copy-start = (bf16[1,8,1024]{2,1,0:T(8,128)(2,1)S(1)}, bf16[1,8,1024]{2,1,0:T(8,128)(2,1)}, u32[]{:S(2)}) copy-start(bf16[1,8,1024]{2,1,0:T(8,128)(2,1)} %param.17) | copy-start | bytes 49156
  6.5 175.0 %all-gather.5.cloned.1.call-start = ((), (), s32[]{:S(2)}) async-start(), calls=%async_computation.1 | async-start | bytes 1114112 | tf_op jit(solution)/shard_map/all_gather | solution.py:177
  10.3 11.4 %copy-start.2 = (bf16[1,4096,160]{1,2,0:T(8,128)(2,1)S(1)}, bf16[1,4096,160]{1,2,0:T(8,128)(2,1)}, u32[]{:S(2)}) copy-start(bf16[1,4096,160]{1,2,0:T(8,128)(2,1)} %param.12) | copy-start | bytes 3932164
  10.3 13.8 %copy-start.3 = (bf16[1,16,8]{1,2,0:T(8,128)(2,1)S(1)}, bf16[1,16,8]{1,2,0:T(8,128)(2,1)}, u32[]{:S(2)}) copy-start(bf16[1,16,8]{1,2,0:T(8,128)(2,1)} %param.14) | copy-start | bytes 772
  10.3 13.9 %copy-start.1 = (bf16[160,1024]{1,0:T(8,128)(2,1)S(1)}, bf16[160,1024]{1,0:T(8,128)(2,1)}, u32[]{:S(2)}) copy-start(bf16[160,1024]{1,0:T(8,128)(2,1)} %param.18) | copy-start | bytes 983044
  123.4 68.7 %reduce-scatter.2.cloned.1.call-start = ((), (), s32[]{:S(2)}) async-start(), calls=%async_computation.2 | async-start | bytes 393216 | tf_op jit(solution)/shard_map/reduce_scatter | solution.py:178
Sparse Core Ops, SparseCore 0:
  123.6 57.9 all-gather.4
  185.7 6.4 reduce-scatter.1
where the time goes:
time: 200 us; the launch traced here: 199 us
  waiting for transfers between devices  64.7 us (32%)
  local copies, waits for them, and re-layouts  42.2 us (21%)
  matrix products  38.9 us (19%)
  other arithmetic  31 us (16%)
  between operations  14.2 us (7%)
  blocking collectives  5.89 us (3%)
  loops' own time  2.05 us (1%)
    all_gather x1, waiting for transfers between devices, body(): all_rows = lax.all_gather(attended, 'group', axis=0, tiled=True)  58.1 us
    dot_general x16, matrix products, attend_block(): jnp.dot(latent, key_factor, preferred_element_type=jnp.float32)  19.1 us
    dynamic_slice x16, local copies, waits for them, and re-layouts, advance(): code_block = lax.dynamic_slice_in_dim(code_rows, block_index * BLK, BLK, 0)  17.3 us
    unnamed x12, local copies, waits for them, and re-layouts  15.4 us
    lt x16, other arithmetic, attend_block(): valid_mask = (positions < length)[None, None, None, :]  10.5 us
    cos x16, other arithmetic, rotate(): cosine = jnp.cos(angles)[:, None, :]  8.53 us
    dot_general x16, matrix products, attend_block(): jnp.einsum('onvs,xns->onvx', query_matrix_rows, rotary_applied, preferred...  8.17 us
    reduce_scatter x1, waiting for transfers between devices, body(): lax.psum_scatter(jnp.dot(all_rows, out_weight, preferred_element_type=jnp...  6.63 us
  transfers between devices with their start and end apart: 2, of which 2 were waited for; matrix products, arithmetic and copies ran while one was open for 0% of the time, Pallas kernels for 0%

commit v1 on v0

v1 whole, which is shorter than its diff:
```python
import functools
import math

import jax
import jax.numpy as jnp
import numpy as np
from jax import lax
from jax.experimental import pallas as pl
from jax.experimental.pallas import tpu as pltpu
from jax.sharding import PartitionSpec as P

HEADS = 64
KV_HEADS = 8
GROUPS = HEADS // KV_HEADS
HEAD_DIM = 128
HALF = HEAD_DIM // 2
BLK = 256
Q_TOK = 8
ROWS = Q_TOK * GROUPS
PAIR = 2
CHUNK = 512
ROPE_BASE = 500000.0
NEG_FILL = -1e30
TO_EXP2 = math.log2(math.e) / math.sqrt(HEAD_DIM)
MESH = pl.DeviceIdType.MESH
F32 = jnp.float32
BF16 = jnp.bfloat16


def rope_tables(ctx):
    exponent = -(np.arange(HALF, dtype=np.float64) * 2.0) / HEAD_DIM
    frequency = (ROPE_BASE**exponent).astype(np.float32)
    angles = frequency[:, None] * np.arange(ctx, dtype=np.float32)[None, :]
    angles = angles.astype(np.float64)
    return np.cos(angles).astype(np.float32), np.sin(angles).astype(np.float32)


def stacked_rows(block):
    wide = block.astype(F32)
    return jnp.concatenate(
        [wide[:, g * HEAD_DIM : (g + 1) * HEAD_DIM] for g in range(GROUPS)], axis=0
    ).astype(BF16)


def padded(block):
    wide = block.astype(F32)
    blank = jnp.zeros((HEAD_DIM - Q_TOK, HEAD_DIM), F32)
    return jnp.concatenate([wide, blank], axis=0).astype(BF16)


def attend_kernel(
    place, scales, latents, factor, cosine, sine, queries, codes, new_keys, new_values,
    numer, stats, scores,
):
    pair = pl.program_id(0)
    at, length = place[0], place[1]
    own = latents.shape[0]
    base = at * own
    turned = factor[...].astype(F32).T.astype(BF16)
    query = [
        stacked_rows(queries[:, i * GROUPS * HEAD_DIM : (i + 1) * GROUPS * HEAD_DIM])
        for i in range(PAIR)
    ]
    tops = [jnp.full((ROWS, HEAD_DIM), NEG_FILL, F32) for _ in range(PAIR)]
    for c in range(own // CHUNK):
        span = slice(c * CHUNK, (c + 1) * CHUNK)
        keys = lax.dot_general(
            turned, latents[span, :], (((1,), (1,)), ((), ())), preferred_element_type=F32
        )
        cos, sin = cosine[:, span], sine[:, span]
        position = base + c * CHUNK + lax.broadcasted_iota(jnp.int32, (1, CHUNK), 1)
        valid = position < length
        for i in range(PAIR):
            low = keys[i * HEAD_DIM : i * HEAD_DIM + HALF]
            high = keys[i * HEAD_DIM + HALF : (i + 1) * HEAD_DIM]
            rotated = jnp.concatenate(
                [low * cos - high * sin, high * cos + low * sin], axis=0
            ).astype(BF16)
            score = jnp.dot(query[i], rotated, preferred_element_type=F32)
            score = jnp.where(valid, score, NEG_FILL)
            scores[i, :, span] = score
            for v in range(CHUNK // HEAD_DIM):
                tops[i] = jnp.maximum(tops[i], score[:, v * HEAD_DIM : (v + 1) * HEAD_DIM])
    column = lax.broadcasted_iota(jnp.int32, (ROWS, HEAD_DIM), 1)
    token = lax.broadcasted_iota(jnp.int32, (ROWS, HEAD_DIM), 0) % Q_TOK
    causal = jnp.logical_and(column <= token, at == 0)
    for i in range(PAIR):
        lanes = slice(i * HEAD_DIM, (i + 1) * HEAD_DIM)
        fresh = lax.dot_general(
            query[i], padded(new_keys[:, lanes]), (((1,), (1,)), ((), ())),
            preferred_element_type=F32,
        )
        fresh = jnp.where(causal, fresh, NEG_FILL)
        peak = jnp.max(jnp.maximum(tops[i], fresh), axis=1, keepdims=True) * TO_EXP2
        weight = jnp.where(causal, jnp.exp2(fresh * TO_EXP2 - peak), 0.0)
        total = weight
        part = jnp.dot(weight.astype(BF16), padded(new_values[:, lanes]), preferred_element_type=F32)
        for b in range(own // BLK):
            span = slice(b * BLK, (b + 1) * BLK)
            weight = jnp.exp2(scores[i, :, span] * TO_EXP2 - peak)
            for v in range(BLK // HEAD_DIM):
                total = total + weight[:, v * HEAD_DIM : (v + 1) * HEAD_DIM]
            product = jnp.dot(weight.astype(BF16), codes[span, lanes], preferred_element_type=F32)
            part = part + product * scales[b, pair * PAIR + i]
        total = jnp.sum(total, axis=1, keepdims=True)
        numer[i] = part
        stats[i] = jnp.where(column < HALF, peak, total)


def attend(place, scales, latents, factor, queries, codes, new_keys, new_values, ctx):
    own, rank = latents.shape
    cosine, sine = rope_tables(ctx)
    wide = PAIR * HEAD_DIM
    vmem = lambda shape, index: pl.BlockSpec(shape, index)
    shape = jax.ShapeDtypeStruct((KV_HEADS, ROWS, HEAD_DIM), F32)
    return pl.pallas_call(
        attend_kernel,
        out_shape=(shape, shape),
        grid_spec=pltpu.PrefetchScalarGridSpec(
            num_scalar_prefetch=2,
            grid=(KV_HEADS // PAIR,),
            in_specs=[
                vmem((own, rank), lambda j, p, s: (0, 0)),
                vmem((rank, wide), lambda j, p, s: (0, j)),
                vmem((HALF, own), lambda j, p, s: (0, p[0])),
                vmem((HALF, own), lambda j, p, s: (0, p[0])),
                vmem((Q_TOK, GROUPS * wide), lambda j, p, s: (0, j)),
                vmem((own, wide), lambda j, p, s: (0, j)),
                vmem((Q_TOK, wide), lambda j, p, s: (0, j)),
                vmem((Q_TOK, wide), lambda j, p, s: (0, j)),
            ],
            out_specs=[
                vmem((PAIR, ROWS, HEAD_DIM), lambda j, p, s: (j, 0, 0)),
                vmem((PAIR, ROWS, HEAD_DIM), lambda j, p, s: (j, 0, 0)),
            ],
            scratch_shapes=[pltpu.VMEM((PAIR, ROWS, own), F32)],
        ),
        compiler_params=pltpu.CompilerParams(vmem_limit_bytes=48 * 1024 * 1024),
        name="attend",
    )(place, scales, latents, factor, jnp.asarray(cosine), jnp.asarray(sine), queries, codes,
      new_keys, new_values)


def lattice(size):
    return {16: (4, 2, 2), 64: (4, 4, 4)}.get(size, (size, 1, 1))


def gather_chain(buffer, order, axis, sizes, spot, group_of, send, recv):
    size, mine = sizes[axis], spot[axis]

    def block(index):
        where = []
        for a in range(3):
            if a == axis:
                where.append(index)
            elif a in order:
                where.append(slice(None))
            else:
                where.append(spot[a])
        return buffer.at[tuple(where)]

    def neighbour(step):
        there = list(spot)
        there[axis] = there[axis] + step
        return group_of(there)

    def copy(index, direction, step):
        to = neighbour(1 if direction == 0 else -1)
        return pltpu.make_async_remote_copy(
            src_ref=block(index),
            dst_ref=block(index),
            send_sem=send.at[axis, direction, step],
            recv_sem=recv.at[axis, direction, step],
            device_id=(to, lax.axis_index("kv")),
            device_id_type=MESH,
        )

    up = lambda s: jnp.logical_and(mine - s >= 0, mine < size - 1)
    down = lambda s: jnp.logical_and(mine + s < size, mine > 0)

    def begin(s):
        @pl.when(up(s))
        def _():
            copy(mine - s, 0, s).start()

        @pl.when(down(s))
        def _():
            copy(mine + s, 1, s).start()

    def arrive(s):
        @pl.when(mine - 1 - s >= 0)
        def _():
            copy(mine - 1 - s, 0, s).wait_recv()

        @pl.when(mine + 1 + s < size)
        def _():
            copy(mine + 1 + s, 1, s).wait_recv()

    def finish(s):
        @pl.when(up(s))
        def _():
            copy(mine - s, 0, s).wait_send()

        @pl.when(down(s))
        def _():
            copy(mine + s, 1, s).wait_send()

    return size - 1, begin, arrive, finish


def project_kernel(
    sizes, numer, stats, weight_hbm, out,
    weight, got_numer, got_stats, buffer, rows, partial, got_partial,
    weight_sem, pair_send, pair_recv, send, recv,
):
    at = lax.axis_index("kv")
    other = 1 - at
    me = lax.axis_index("group")
    z_size, y_size, x_size = sizes
    spot = [me // (y_size * x_size), me // x_size % y_size, me % x_size]
    group_of = lambda s: (s[0] * y_size + s[1]) * x_size + s[2]

    barrier = pltpu.get_barrier_semaphore()
    pl.semaphore_signal(barrier, inc=1, device_id=(me, other), device_id_type=MESH)
    expected = 1
    for axis in range(3):
        for step in (-1, 1):
            if sizes[axis] == 1:
                continue
            inside = jnp.logical_and(spot[axis] + step >= 0, spot[axis] + step < sizes[axis])
            there = list(spot)
            there[axis] = there[axis] + step

            @pl.when(inside)
            def _(there=there):
                pl.semaphore_signal(
                    barrier, inc=1, device_id=(group_of(there), at), device_id_type=MESH
                )

            expected = expected + inside.astype(jnp.int32)
    load = pltpu.make_async_copy(weight_hbm, weight, weight_sem)
    load.start()
    pl.semaphore_wait(barrier, expected)

    half_heads = KV_HEADS // 2
    pair_copy = lambda n, src, dst: pltpu.make_async_remote_copy(
        src_ref=src, dst_ref=dst, send_sem=pair_send.at[n], recv_sem=pair_recv.at[n],
        device_id=(me, other), device_id_type=MESH,
    )
    theirs = pl.ds(other * half_heads, half_heads)
    first = pair_copy(0, stats.at[theirs], got_stats)
    second = pair_copy(1, numer.at[theirs], got_numer)
    first.start()
    second.start()
    first.wait()
    second.wait()
    for k in range(half_heads):
        mine_stat, their_stat = stats[at * half_heads + k], got_stats[k]
        mine_peak, mine_total = mine_stat[:, :1], mine_stat[:, HALF : HALF + 1]
        their_peak, their_total = their_stat[:, :1], their_stat[:, HALF : HALF + 1]
        peak = jnp.maximum(mine_peak, their_peak)
        mine_scale, their_scale = jnp.exp2(mine_peak - peak), jnp.exp2(their_peak - peak)
        total = mine_total * mine_scale + their_total * their_scale
        joined = numer[at * half_heads + k] * mine_scale + got_numer[k] * their_scale
        buffer[k // 2, spot[0], spot[1], spot[2], (k % 2) * ROWS : (k % 2 + 1) * ROWS] = (
            joined / total
        ).astype(BF16)

    orders = ((0, 1, 2), (0, 2, 1))
    for stage in range(3):
        chains = [
            gather_chain(
                buffer.at[c], orders[c][:stage], orders[c][stage], sizes, spot, group_of,
                send.at[c], recv.at[c],
            )
            for c in range(2)
        ]
        for s in range(max(chain[0] for chain in chains)):
            for steps, begin, arrive, finish in chains:
                if s < steps:
                    begin(s)
            for steps, begin, arrive, finish in chains:
                if s < steps:
                    arrive(s)
        for steps, begin, arrive, finish in chains:
            for s in range(steps):
                finish(s)

    members = z_size * y_size * x_size
    for k in range(half_heads):
        block = buffer[k // 2, :, :, :, (k % 2) * ROWS : (k % 2 + 1) * ROWS, :]
        block = block.reshape(members, ROWS, HEAD_DIM).astype(F32)
        for g in range(GROUPS):
            piece = block[:, g * Q_TOK : (g + 1) * Q_TOK, :]
            feature = (k * GROUPS + g) * HEAD_DIM
            rows[:, feature : feature + HEAD_DIM] = piece.reshape(
                members * Q_TOK, HEAD_DIM
            ).astype(BF16)
    load.wait()
    partial[...] = jnp.dot(rows[...], weight[...], preferred_element_type=F32)
    half_rows = members * Q_TOK // 2
    last = pair_copy(2, partial.at[pl.ds(other * half_rows, half_rows)], got_partial)
    last.start()
    last.wait()
    out[...] = partial[pl.ds(at * half_rows, half_rows)] + got_partial[...]


def project(numer, stats, out_weight, members):
    depth, columns = out_weight.shape
    sizes = lattice(members)
    half = KV_HEADS // 2
    count = members * Q_TOK
    longest = max(max(sizes) - 1, 1)
    return pl.pallas_call(
        functools.partial(project_kernel, sizes),
        out_shape=jax.ShapeDtypeStruct((count // 2, columns), F32),
        in_specs=[
            pl.BlockSpec(memory_space=pltpu.VMEM),
            pl.BlockSpec(memory_space=pltpu.VMEM),
            pl.BlockSpec(memory_space=pl.ANY),
        ],
        out_specs=pl.BlockSpec(memory_space=pltpu.VMEM),
        scratch_shapes=[
            pltpu.VMEM((depth, columns), BF16),
            pltpu.VMEM((half, ROWS, HEAD_DIM), F32),
            pltpu.VMEM((half, ROWS, HEAD_DIM), F32),
            pltpu.VMEM((2, *sizes, half // 2 * ROWS, HEAD_DIM), BF16),
            pltpu.VMEM((count, depth), BF16),
            pltpu.VMEM((count, columns), F32),
            pltpu.VMEM((count // 2, columns), F32),
            pltpu.SemaphoreType.DMA,
            pltpu.SemaphoreType.DMA((3,)),
            pltpu.SemaphoreType.DMA((3,)),
            pltpu.SemaphoreType.DMA((2, 3, 2, longest)),
            pltpu.SemaphoreType.DMA((2, 3, 2, longest)),
        ],
        compiler_params=pltpu.CompilerParams(
            collective_id=0, has_side_effects=True, vmem_limit_bytes=48 * 1024 * 1024
        ),
        name="project",
    )(numer, stats, out_weight)


def body(lengths, latents, codes, scales, queries, new_keys, new_values, key_factor, out_weight):
    at = lax.axis_index("kv")
    ctx = latents.shape[1] * lax.axis_size("kv")
    place = jnp.stack([at.astype(jnp.int32), lengths[0]])
    numer, stats = attend(
        place, scales[0].astype(F32), latents[0], key_factor, queries[0], codes[0],
        new_keys[0], new_values[0], ctx,
    )
    return project(numer, stats, out_weight, lax.axis_size("group"))


def solution(mesh):
    placed = (
        P("group"),
        P("group", "kv", None),
        P("group", "kv", None),
        P("group", "kv", None),
        P("group", None, None),
        P("group", None, None),
        P("group", None, None),
        P(),
        P("kv", "group"),
    )
    return jax.shard_map(
        body, mesh=mesh, in_specs=placed, out_specs=P("kv", "group"), check_vma=False
    )
```

time: 200 us -> 54 us (0.27)
  waiting for transfers between devices: 64.7 us -> 0 us
  Pallas kernels: 0 us -> 46.8 us
  matrix products: 38.9 us -> 0 us
  local copies, waits for them, and re-layouts: 42.2 us -> 5.42 us
  other arithmetic: 31 us -> 0.76 us
  between operations: 14.2 us -> 0.78 us
  blocking collectives: 5.89 us -> 0 us
  loops' own time: 2.05 us -> 0 us
    all_gather x1 -> x0, waiting for transfers between devices: 58.1 us -> none  [body(): all_rows = lax.all_gather(attended, 'group', axis=0, tiled=True)]
    pallas_call x0 -> x2, Pallas kernels: none -> 46.8 us  [the longest x1 29.2 us: project(): pl.pallas_call(functools.partial(project_kernel, sizes), out_shape=jax.Sh...]
    dot_general x51 -> x0, matrix products: 38.9 us -> none  [the longest x16 19.1 us: attend_block(): jnp.dot(latent, key_factor, preferred_element_type=jnp.float32)]
    dynamic_slice x21 -> x0, local copies, waits for them, and re-layouts: 17.4 us -> none  [the longest x16 17.3 us: advance(): code_block = lax.dynamic_slice_in_dim(code_rows, block_index * BLK, BLK, 0)]
    lt x16 -> x0, other arithmetic: 10.5 us -> none  [attend_block(): valid_mask = (positions < length)[None, None, None, :]]
    unnamed x12 -> x14, local copies, waits for them, and re-layouts: 15.4 us -> 5.35 us
    cos x16 -> x0, other arithmetic: 8.53 us -> none  [rotate(): cosine = jnp.cos(angles)[:, None, :]]
    reduce_scatter x1 -> x0, waiting for transfers between devices: 6.63 us -> none  [body(): lax.psum_scatter(jnp.dot(all_rows, out_weight, preferred_element_type=jnp...]
  transfers between devices with their start and end apart: 2 -> 0, of which waited for: 2 -> 0; matrix products, arithmetic and copies ran while one was open for 0% -> 0% of each run, Pallas kernels for 0% -> 0%
where the time goes in v1:
time: 54 us; the launch traced here: 53.7 us
  Pallas kernels  46.8 us (87%)
  local copies, waits for them, and re-layouts  5.42 us (10%)
  between operations  0.78 us (1%)
  other arithmetic  0.76 us (1%)
    pallas_call x1, Pallas kernels, project(): pl.pallas_call(functools.partial(project_kernel, sizes), out_shape=jax.Sh...  29.2 us
    pallas_call x1, Pallas kernels, attend(): pl.pallas_call(attend_kernel, out_shape=(shape, shape), grid_spec=pltpu.P...  17.6 us
    unnamed x14, local copies, waits for them, and re-layouts  5.35 us

profile of v1, /device:TPU:0, one launch (start us, length us, event | category | flops | bytes accessed | tf_op | source)
XLA Modules:
  0.0 53.7 jit_solution(6704170899495732196)
XLA Ops:
  0.0 0.0 copy-start.2
  0.0 0.0 copy-start.5
  0.0 0.0 copy-start.4
  0.0 0.0 copy-start.3
  0.7 0.1 pad_add_fusion.place
  0.8 0.7 %bitcast_convert_fusion = f32[16,8]{0,1:T(8,128)S(1)} fusion(bf16[1,16,8]{1,2,0:T(8,128)(2,1)} %param.14), kind=kLoop, calls=%fused_computation | loop fusion | flops 128 | bytes 768 | tf_op jit(solution)/shard_map/convert_element_type | solution.py:349
  1.5 0.1 copy.13.scales
  1.5 3.1 %copy.12 = bf16[1,4096,160]{2,1,0:T(8,128)(2,1)S(1)} copy(bf16[1,4096,160]{1,2,0:T(8,128)(2,1)} %param.12) | data formatting | bytes 2621440 | tf_op args[1]
  4.6 0.0 copy-done.2
  4.7 0.0 copy-done.5
  4.7 0.0 copy-done.4
  4.7 0.0 copy-done.3
  4.7 0.0 copy-start.1
  4.7 1.6 %copy-done.1 = f32[64,8192]{1,0:T(8,128)S(1)} copy-done((f32[64,8192]{1,0:T(8,128)S(1)}, f32[64,8192]{1,0:T(8,128)}, u32[]{:S(2)}) %copy-start.1) | copy-done | bytes 2097176
  6.3 0.0 copy-start
  6.3 17.6 %attend.1 = (f32[8,64,128]{2,1,0:T(8,128)S(1)}, f32[8,64,128]{2,1,0:T(8,128)S(1)}) custom-call(s32[2]{0:T(128)S(1)} %pad_add_fusion.place, f32[16,8]{1,0:T(8,128)S(1)} %copy.13.scales, bf16[4096,160]{1,0:T(8,128)(2,1)S(1)} %bitcast.9, bf16[160,1024]{1,0:T(8,128)(2,1)S(1)} %copy-done.2, f32[64,8192]{1,0:T(8,128)S(1)} %copy-done.1, ...), custom_call_target="tpu_custom_call" | custom-call | tf_op jit(solution)/shard_map/attend/pallas_call | solution.py:116
  23.9 0.0 copy-done
  23.9 29.2 %project.1 = f32[64,512]{1,0:T(8,128)S(1)} custom-call(f32[8,64,128]{2,1,0:T(8,128)S(1)} %get-tuple-element.7.numer, f32[8,64,128]{2,1,0:T(8,128)S(1)} %get-tuple-element.8.stats, bf16[4096,512]{1,0:T(8,128)(2,1)S(1)} %copy-done), custom_call_target="tpu_custom_call" | custom-call | tf_op jit(solution)/shard_map/project/pallas_call | solution.py:314
  53.1 0.7 %copy.16 = f32[64,512]{1,0:T(8,128)} copy(f32[64,512]{1,0:T(8,128)S(1)} %project.1) | data formatting | bytes 262144
Async XLA Ops:
  0.0 4.6 %copy-start.2 = (bf16[160,1024]{1,0:T(8,128)(2,1)S(1)}, bf16[160,1024]{1,0:T(8,128)(2,1)}, u32[]{:S(2)}) copy-start(bf16[160,1024]{1,0:T(8,128)(2,1)} %factor.1) | copy-start | bytes 983044
  0.0 4.7 %copy-start.5 = (bf16[1,8,1024]{2,1,0:T(8,128)(2,1)S(1)}, bf16[1,8,1024]{2,1,0:T(8,128)(2,1)}, u32[]{:S(2)}) copy-start(bf16[1,8,1024]{2,1,0:T(8,128)(2,1)} %param.17) | copy-start | bytes 49156
  0.0 4.7 %copy-start.4 = (bf16[1,8,1024]{2,1,0:T(8,128)(2,1)S(1)}, bf16[1,8,1024]{2,1,0:T(8,128)(2,1)}, u32[]{:S(2)}) copy-start(bf16[1,8,1024]{2,1,0:T(8,128)(2,1)} %param.16) | copy-start | bytes 49156
  0.0 4.7 %copy-start.3 = (bf16[1,8,8192]{2,1,0:T(8,128)(2,1)S(1)}, bf16[1,8,8192]{2,1,0:T(8,128)(2,1)}, u32[]{:S(2)}) copy-start(bf16[1,8,8192]{2,1,0:T(8,128)(2,1)} %param.15) | copy-start | bytes 393220
  4.7 1.6 %copy-start.1 = (f32[64,8192]{1,0:T(8,128)S(1)}, f32[64,8192]{1,0:T(8,128)}, u32[]{:S(2)}) copy-start(f32[64,8192]{1,0:T(8,128)} %constant.8.clone.cosine) | copy-start | bytes 6291460
  6.3 17.6 %copy-start = (bf16[4096,512]{1,0:T(8,128)(2,1)S(1)}, bf16[4096,512]{1,0:T(8,128)(2,1)}, u32[]{:S(2)}) copy-start(bf16[4096,512]{1,0:T(8,128)(2,1)} %weight_hbm.1) | copy-start | bytes 12582916

commit v2 on v0

v2 whole, which is shorter than its diff:
```python
import math

import jax
import jax.numpy as jnp
import numpy as np
from jax import lax
from jax.experimental import pallas as pl
from jax.experimental.pallas import tpu as pltpu
from jax.sharding import PartitionSpec as P

HEADS = 64
KV_HEADS = 8
GROUPS = HEADS // KV_HEADS
HEAD_DIM = 128
HALF = HEAD_DIM // 2
BLK = 256
Q_TOK = 8
ROWS = Q_TOK * GROUPS
PAIR = 2
CHUNK = 512
ROPE_BASE = 500000.0
NEG_FILL = -1e30
TO_EXP2 = math.log2(math.e) / math.sqrt(HEAD_DIM)
MESH = pl.DeviceIdType.MESH
F32 = jnp.float32
BF16 = jnp.bfloat16


def rope_tables(ctx):
    exponent = -(np.arange(HALF, dtype=np.float64) * 2.0) / HEAD_DIM
    frequency = (ROPE_BASE**exponent).astype(np.float32)
    angles = frequency[:, None] * np.arange(ctx, dtype=np.float32)[None, :]
    angles = angles.astype(np.float64)
    return np.cos(angles).astype(np.float32), np.sin(angles).astype(np.float32)


def stacked_rows(block):
    wide = block.astype(F32)
    return jnp.concatenate(
        [wide[:, g * HEAD_DIM : (g + 1) * HEAD_DIM] for g in range(GROUPS)], axis=0
    ).astype(BF16)


def padded(block):
    wide = block.astype(F32)
    blank = jnp.zeros((HEAD_DIM - Q_TOK, HEAD_DIM), F32)
    return jnp.concatenate([wide, blank], axis=0).astype(BF16)


def step_kernel(
    length, scales, latents_hbm, codes_hbm, cosine_hbm, sine_hbm, queries, new_keys, new_values,
    factor, weight_hbm, out,
    latents, codes, cosine, sine, weight, scores, mine, theirs, got, buffer, rows, partial,
    got_partial,
    piece_sem, codes_sem, weight_sem, pair_send, pair_recv, last_send, last_recv, send, recv,
):
    at = lax.axis_index("kv")
    other = 1 - at
    me = lax.axis_index("group")
    own = latents.shape[1]
    base = at * own
    rounds = buffer.shape[0]
    levels = buffer.ndim - 4
    members = 2**levels
    bits = [me // 2**b % 2 for b in range(levels)]
    partner = [me + (1 - 2 * bits[b]) * 2**b for b in range(levels)]
    orders = [list(range(levels))[::-1], list(range(2, levels))[::-1] + [0, 1]]
    pieces = piece_sem.shape[1]
    wide = own // pieces

    def piece_copies(n):
        span = pl.ds(n * wide, wide)
        there = pl.ds(pl.multiple_of(base + n * wide, wide), wide)
        return [
            pltpu.make_async_copy(latents_hbm.at[:, span], latents.at[:, span], piece_sem.at[0, n]),
            pltpu.make_async_copy(cosine_hbm.at[:, there], cosine.at[:, span], piece_sem.at[1, n]),
            pltpu.make_async_copy(sine_hbm.at[:, there], sine.at[:, span], piece_sem.at[2, n]),
        ]

    def head_of(r, i):
        return (at if i == 0 else other) * rounds + r

    def codes_copies(r):
        result = []
        for i in range(PAIR):
            lanes = pl.ds(pl.multiple_of(head_of(r, i) * HEAD_DIM, HEAD_DIM), HEAD_DIM)
            result.append(
                pltpu.make_async_copy(codes_hbm.at[:, lanes], codes.at[r, i], codes_sem.at[r, i])
            )
        return result

    load = pltpu.make_async_copy(weight_hbm, weight, weight_sem)
    for n in range(pieces):
        for copy in piece_copies(n):
            copy.start()
    for r in range(rounds):
        for copy in codes_copies(r):
            copy.start()
    load.start()

    barrier = pltpu.get_barrier_semaphore()
    pl.semaphore_signal(barrier, inc=1, device_id=(me, other), device_id_type=MESH)
    for b in range(levels):
        pl.semaphore_signal(barrier, inc=1, device_id=(partner[b], at), device_id_type=MESH)
    pl.semaphore_wait(barrier, levels + 1)

    def pair_copy(r):
        return pltpu.make_async_remote_copy(
            src_ref=theirs.at[r], dst_ref=got.at[r], send_sem=pair_send.at[r],
            recv_sem=pair_recv.at[r], device_id=(me, other), device_id_type=MESH,
        )

    def gather_copy(r, half, step):
        order = orders[half]
        b = order[step]
        where = [slice(None)] * levels
        for rest in order[step:]:
            where[levels - 1 - rest] = bits[rest]
        block = buffer.at[(r, half, *where)]
        return pltpu.make_async_remote_copy(
            src_ref=block, dst_ref=block, send_sem=send.at[r, half, step],
            recv_sem=recv.at[r, half, step], device_id=(partner[b], at), device_id_type=MESH,
        )

    def combine(r):
        pair_copy(r).wait()
        mine_stat, their_stat = mine[r, 1], got[r, 1]
        mine_peak, mine_total = mine_stat[:, :1], mine_stat[:, HALF : HALF + 1]
        their_peak, their_total = their_stat[:, :1], their_stat[:, HALF : HALF + 1]
        peak = jnp.maximum(mine_peak, their_peak)
        mine_scale, their_scale = jnp.exp2(mine_peak - peak), jnp.exp2(their_peak - peak)
        total = mine_total * mine_scale + their_total * their_scale
        joined = (mine[r, 0] * mine_scale + got[r, 0] * their_scale) / total
        spot = bits[::-1]
        for half in range(2):
            part = joined[half * ROWS // 2 : (half + 1) * ROWS // 2]
            buffer[(r, half, *spot)] = part.astype(BF16)
            gather_copy(r, half, 0).start()

    def relay(r, step):
        for half in range(2):
            gather_copy(r, half, step).wait()
            if step + 1 < levels:
                gather_copy(r, half, step + 1).start()

    def collect(r):
        relay(r, levels - 1)
        for half in range(2):
            block = buffer[r, half].reshape(members, ROWS // 2, HEAD_DIM).astype(F32)
            for g in range(GROUPS // 2):
                piece = block[:, g * Q_TOK : (g + 1) * Q_TOK, :]
                feature = (half * GROUPS // 2 + g) * HEAD_DIM
                rows[:, feature : feature + HEAD_DIM] = piece.reshape(
                    members * Q_TOK, HEAD_DIM
                ).astype(BF16)

    depth = GROUPS * HEAD_DIM

    def multiply(r, span):
        layer = weight[pl.ds(pl.multiple_of(r * depth, depth), depth), :]
        partial[span, :] += jnp.dot(rows[span, :], layer, preferred_element_type=F32)

    def whole_product(r):
        collect(r)

        @pl.when(r == 0)
        def _():
            load.wait()

        multiply(r, slice(None))

    column = lax.broadcasted_iota(jnp.int32, (ROWS, HEAD_DIM), 1)
    token = lax.broadcasted_iota(jnp.int32, (ROWS, HEAD_DIM), 0) % Q_TOK
    causal = jnp.logical_and(column <= token, at == 0)
    limit = length[0] - base

    def one_round(r, _):
        def hook(action):
            @pl.when(r > 0)
            def _():
                action(r - 1)

        lanes = [
            pl.ds(pl.multiple_of(head_of(r, i) * HEAD_DIM, HEAD_DIM), HEAD_DIM)
            for i in range(PAIR)
        ]
        turned = jnp.concatenate(
            [factor[:, lanes[i]].astype(F32).T for i in range(PAIR)], axis=0
        ).astype(BF16)
        query = [
            stacked_rows(queries[:, pl.ds(pl.multiple_of(head_of(r, i) * depth, depth), depth)])
            for i in range(PAIR)
        ]
        tops = [jnp.full((ROWS, HEAD_DIM), NEG_FILL, F32) for _ in range(PAIR)]
        for c in range(own // CHUNK):
            span = slice(c * CHUNK, (c + 1) * CHUNK)
            if c * CHUNK % wide == 0:

                @pl.when(r == 0)
                def _(n=c * CHUNK // wide):
                    for copy in piece_copies(n):
                        copy.wait()

            keys = jnp.dot(turned, latents[:, span], preferred_element_type=F32)
            cos, sin = cosine[:, span], sine[:, span]
            valid = c * CHUNK + lax.broadcasted_iota(jnp.int32, (1, CHUNK), 1) < limit
            for i in range(PAIR):
                low = keys[i * HEAD_DIM : i * HEAD_DIM + HALF]
                high = keys[i * HEAD_DIM + HALF : (i + 1) * HEAD_DIM]
                rotated = jnp.concatenate(
                    [low * cos - high * sin, high * cos + low * sin], axis=0
                ).astype(BF16)
                score = jnp.dot(query[i], rotated, preferred_element_type=F32)
                score = jnp.where(valid, score, NEG_FILL)
                scores[i, :, span] = score
                for v in range(CHUNK // HEAD_DIM):
                    tops[i] = jnp.maximum(tops[i], score[:, v * HEAD_DIM : (v + 1) * HEAD_DIM])
            if c == 1:
                hook(combine)
            if c >= 3 and c % 2 == 1 and (c - 3) // 2 < levels - 2:
                hook(lambda q, step=(c - 3) // 2: relay(q, step))
        for step in range(min(levels - 2, (own // CHUNK - 2) // 2), levels - 1):
            hook(lambda q, step=step: relay(q, step))
        for copy in codes_copies(r):
            copy.wait()
        for i in (1, 0):
            fresh = lax.dot_general(
                query[i], padded(new_keys[:, lanes[i]]), (((1,), (1,)), ((), ())),
                preferred_element_type=F32,
            )
            fresh = jnp.where(causal, fresh, NEG_FILL)
            peak = jnp.max(jnp.maximum(tops[i], fresh), axis=1, keepdims=True) * TO_EXP2
            weights = jnp.where(causal, jnp.exp2(fresh * TO_EXP2 - peak), 0.0)
            total = weights
            part = jnp.dot(
                weights.astype(BF16), padded(new_values[:, lanes[i]]), preferred_element_type=F32
            )
            for b in range(own // BLK):
                span = slice(b * BLK, (b + 1) * BLK)
                weights = jnp.exp2(scores[i, :, span] * TO_EXP2 - peak)
                for v in range(BLK // HEAD_DIM):
                    total = total + weights[:, v * HEAD_DIM : (v + 1) * HEAD_DIM]
                product = jnp.dot(
                    weights.astype(BF16), codes[r, i, span, :], preferred_element_type=F32
                )
                part = part + product * scales[head_of(r, i), b]
            total = jnp.sum(total, axis=1, keepdims=True)
            keep = mine if i == 0 else theirs
            keep[r, 0] = part
            keep[r, 1] = jnp.where(column < HALF, peak, total)
            if i == 1:
                pair_copy(r).start()
        hook(whole_product)
        return 0

    partial[...] = jnp.zeros_like(partial)
    lax.fori_loop(0, rounds, one_round, 0)
    final = rounds - 1
    combine(final)
    for step in range(levels - 1):
        relay(final, step)
    collect(final)
    half_rows = members * Q_TOK // 2
    half_of = lambda n: pl.ds(pl.multiple_of(n * half_rows, half_rows), half_rows)
    multiply(final, half_of(other))
    last = pltpu.make_async_remote_copy(
        src_ref=partial.at[half_of(other)], dst_ref=got_partial, send_sem=last_send,
        recv_sem=last_recv, device_id=(me, other), device_id_type=MESH,
    )
    last.start()
    multiply(final, half_of(at))
    last.wait()
    out[...] = partial[half_of(at)] + got_partial[...]


def body(lengths, latents, codes, scales, queries, new_keys, new_values, key_factor, out_weight):
    own, rank = latents.shape[1:]
    cosine, sine = rope_tables(own * lax.axis_size("kv"))
    members = lax.axis_size("group")
    levels = members.bit_length() - 1
    assert members == 2**levels and lax.axis_size("kv") == 2
    depth, columns = out_weight.shape
    rounds = KV_HEADS // 2
    count = members * Q_TOK
    pieces = 4
    anywhere = pl.BlockSpec(memory_space=pl.ANY)
    scalar = pl.BlockSpec(memory_space=pltpu.SMEM)
    near = pl.BlockSpec(memory_space=pltpu.VMEM)
    dma = pltpu.SemaphoreType.DMA
    return pl.pallas_call(
        step_kernel,
        out_shape=jax.ShapeDtypeStruct((count // 2, columns), F32),
        in_specs=[scalar, scalar] + [anywhere] * 4 + [near] * 4 + [anywhere],
        out_specs=near,
        scratch_shapes=[
            pltpu.VMEM((rank, own), BF16),
            pltpu.VMEM((rounds, PAIR, own, HEAD_DIM), BF16),
            pltpu.VMEM((HALF, own), F32),
            pltpu.VMEM((HALF, own), F32),
            pltpu.VMEM((depth, columns), BF16),
            pltpu.VMEM((PAIR, ROWS, own), F32),
            pltpu.VMEM((rounds, 2, ROWS, HEAD_DIM), F32),
            pltpu.VMEM((rounds, 2, ROWS, HEAD_DIM), F32),
            pltpu.VMEM((rounds, 2, ROWS, HEAD_DIM), F32),
            pltpu.VMEM((rounds, 2, *[2] * levels, ROWS // 2, HEAD_DIM), BF16),
            pltpu.VMEM((count, GROUPS * HEAD_DIM), BF16),
            pltpu.VMEM((count, columns), F32),
            pltpu.VMEM((count // 2, columns), F32),
            dma((3, pieces)),
            dma((rounds, PAIR)),
            dma,
            dma((rounds,)),
            dma((rounds,)),
            dma,
            dma,
            dma((rounds, 2, levels)),
            dma((rounds, 2, levels)),
        ],
        compiler_params=pltpu.CompilerParams(
            collective_id=0, has_side_effects=True, vmem_limit_bytes=56 * 1024 * 1024
        ),
        name="decode_step",
    )(lengths, scales[0].astype(F32).T, latents[0].T, codes[0], jnp.asarray(cosine),
      jnp.asarray(sine), queries[0], new_keys[0], new_values[0], key_factor, out_weight)


def solution(mesh):
    placed = (
        P("group"),
        P("group", "kv", None),
        P("group", "kv", None),
        P("group", "kv", None),
        P("group", None, None),
        P("group", None, None),
        P("group", None, None),
        P(),
        P("kv", "group"),
    )
    return jax.shard_map(
        body, mesh=mesh, in_specs=placed, out_specs=P("kv", "group"), check_vma=False
    )
```

time: 200 us -> 69.3 us (0.35)
  Pallas kernels: 0 us -> 65.6 us
  waiting for transfers between devices: 64.7 us -> 0 us
  local copies, waits for them, and re-layouts: 42.2 us -> 1.57 us
  matrix products: 38.9 us -> 0 us
  other arithmetic: 31 us -> 1.28 us
  between operations: 14.2 us -> 0.66 us
  blocking collectives: 5.89 us -> 0 us
  loops' own time: 2.05 us -> 0 us
    pallas_call x0 -> x1, Pallas kernels: none -> 65.6 us  [body(): pl.pallas_call(step_kernel, out_shape=jax.ShapeDtypeStruct((count // 2, c...]
    all_gather x1 -> x0, waiting for transfers between devices: 58.1 us -> none  [body(): all_rows = lax.all_gather(attended, 'group', axis=0, tiled=True)]
    dot_general x51 -> x0, matrix products: 38.9 us -> none  [the longest x16 19.1 us: attend_block(): jnp.dot(latent, key_factor, preferred_element_type=jnp.float32)]
    dynamic_slice x21 -> x0, local copies, waits for them, and re-layouts: 17.4 us -> none  [the longest x16 17.3 us: advance(): code_block = lax.dynamic_slice_in_dim(code_rows, block_index * BLK, BLK, 0)]
    unnamed x12 -> x1, local copies, waits for them, and re-layouts: 15.4 us -> 1.57 us
    lt x16 -> x0, other arithmetic: 10.5 us -> none  [attend_block(): valid_mask = (positions < length)[None, None, None, :]]
    cos x16 -> x0, other arithmetic: 8.53 us -> none  [rotate(): cosine = jnp.cos(angles)[:, None, :]]
    reduce_scatter x1 -> x0, waiting for transfers between devices: 6.63 us -> none  [body(): lax.psum_scatter(jnp.dot(all_rows, out_weight, preferred_element_type=jnp...]
  transfers between devices with their start and end apart: 2 -> 0, of which waited for: 2 -> 0; matrix products, arithmetic and copies ran while one was open for 0% -> 0% of each run, Pallas kernels for 0% -> 0%
where the time goes in v2:
time: 69.3 us; the launch traced here: 69.2 us
  Pallas kernels  65.6 us (95%)
  local copies, waits for them, and re-layouts  1.57 us (2%)
  other arithmetic  1.28 us (2%)
    pallas_call x1, Pallas kernels, body(): pl.pallas_call(step_kernel, out_shape=jax.ShapeDtypeStruct((count // 2, c...  65.6 us
    unnamed x1, local copies, waits for them, and re-layouts  1.57 us

profile of v2, /device:TPU:0, one launch (start us, length us, event | category | flops | bytes accessed | tf_op | source)
XLA Modules:
  0.0 69.2 jit_solution(7273853576156478036)
XLA Ops:
  0.7 1.3 %convert_bitcast_fusion.scales = f32[8,16]{1,0:T(8,128)} fusion(bf16[1,16,8]{1,2,0:T(8,128)(2,1)} %param.14), kind=kLoop, calls=%fused_computation | loop fusion | flops 128 | bytes 768 | tf_op jit(solution)/shard_map/transpose | solution.py:323
  1.9 65.6 %decode_step.1 = f32[64,512]{1,0:T(8,128)} custom-call(s32[1]{0:T(128)S(6)} %copy.13.length, f32[8,16]{1,0:T(8,128)} %convert_bitcast_fusion.scales, bf16[160,4096]{1,0:T(8,128)(2,1)} %bitcast.13, bf16[4096,1024]{1,0:T(8,128)(2,1)} %bitcast.12, f32[64,8192]{1,0:T(8,128)} %constant.4.clone.cosine_hbm, f32[64,8192]{1,0:T(8,128)} %constant.5.clone.sine_hbm, ...), custom_call_target="tpu_custom_call" | custom-call | tf_op jit(solution)/shard_map/decode_step/pallas_call | solution.py:290
  67.6 1.6 %copy.14 = f32[64,512]{1,0:T(8,128)} copy(f32[64,512]{1,0:T(8,128)} %decode_step.1) | data formatting | bytes 262144

commit v3 on v2

--- a/solution.py
+++ b/solution.py
@@ -48,11 +48,12 @@
 
 
 def step_kernel(
-    length, scales, latents_hbm, codes_hbm, cosine_hbm, sine_hbm, queries, new_keys, new_values,
-    factor, weight_hbm, out,
-    latents, codes, cosine, sine, weight, scores, mine, theirs, got, buffer, rows, partial,
+    length, latents_hbm, codes_hbm, cosine_hbm, sine_hbm, scales_in, queries, new_keys,
+    new_values, factor, weight_hbm, out,
+    latents, codes, cosine, sine, weight, scales, scores, mine, theirs, got, buffer, rows, partial,
     got_partial,
-    piece_sem, codes_sem, weight_sem, pair_send, pair_recv, last_send, last_recv, send, recv,
+    piece_sem, codes_sem, weight_sem, pair_send, pair_recv, last_send, last_recv,
+    column_send, column_recv, plane_send, plane_recv,
 ):
     at = lax.axis_index("kv")
     other = 1 - at
@@ -60,11 +61,11 @@
     own = latents.shape[1]
     base = at * own
     rounds = buffer.shape[0]
-    levels = buffer.ndim - 4
-    members = 2**levels
-    bits = [me // 2**b % 2 for b in range(levels)]
-    partner = [me + (1 - 2 * bits[b]) * 2**b for b in range(levels)]
-    orders = [list(range(levels))[::-1], list(range(2, levels))[::-1] + [0, 1]]
+    plane, floors = buffer.shape[1:3]
+    members = plane * floors
+    floor, place = me // plane, me % plane
+    above = [((floor + d) % floors) * plane + place for d in range(1, floors)]
+    beside = [floor * plane + (place + d) % plane for d in range(1, plane)]
     pieces = piece_sem.shape[1]
     wide = own // pieces
 
@@ -100,9 +101,10 @@
 
     barrier = pltpu.get_barrier_semaphore()
     pl.semaphore_signal(barrier, inc=1, device_id=(me, other), device_id_type=MESH)
-    for b in range(levels):
-        pl.semaphore_signal(barrier, inc=1, device_id=(partner[b], at), device_id_type=MESH)
-    pl.semaphore_wait(barrier, levels + 1)
+    for peer in above + beside:
+        pl.semaphore_signal(barrier, inc=1, device_id=(peer, at), device_id_type=MESH)
+    pl.semaphore_wait(barrier, len(above) + len(beside) + 1)
+    scales[...] = scales_in[...].astype(F32)
 
     def pair_copy(r):
         return pltpu.make_async_remote_copy(
@@ -110,17 +112,25 @@
             recv_sem=pair_recv.at[r], device_id=(me, other), device_id_type=MESH,
         )
 
-    def gather_copy(r, half, step):
-        order = orders[half]
-        b = order[step]
-        where = [slice(None)] * levels
-        for rest in order[step:]:
-            where[levels - 1 - rest] = bits[rest]
-        block = buffer.at[(r, half, *where)]
-        return pltpu.make_async_remote_copy(
-            src_ref=block, dst_ref=block, send_sem=send.at[r, half, step],
-            recv_sem=recv.at[r, half, step], device_id=(partner[b], at), device_id_type=MESH,
-        )
+    def column_copies(r):
+        block = buffer.at[r, place, floor]
+        return [
+            pltpu.make_async_remote_copy(
+                src_ref=block, dst_ref=block, send_sem=column_send.at[r, d],
+                recv_sem=column_recv.at[r, d], device_id=(peer, at), device_id_type=MESH,
+            )
+            for d, peer in enumerate(above)
+        ]
+
+    def plane_copies(r):
+        block = buffer.at[r, place]
+        return [
+            pltpu.make_async_remote_copy(
+                src_ref=block, dst_ref=block, send_sem=plane_send.at[r, d],
+                recv_sem=plane_recv.at[r, d], device_id=(peer, at), device_id_type=MESH,
+            )
+            for d, peer in enumerate(beside)
+        ]
 
     def combine(r):
         pair_copy(r).wait()
@@ -131,28 +141,27 @@
         mine_scale, their_scale = jnp.exp2(mine_peak - peak), jnp.exp2(their_peak - peak)
         total = mine_total * mine_scale + their_total * their_scale
         joined = (mine[r, 0] * mine_scale + got[r, 0] * their_scale) / total
-        spot = bits[::-1]
-        for half in range(2):
-            part = joined[half * ROWS // 2 : (half + 1) * ROWS // 2]
-            buffer[(r, half, *spot)] = part.astype(BF16)
-            gather_copy(r, half, 0).start()
-
-    def relay(r, step):
-        for half in range(2):
-            gather_copy(r, half, step).wait()
-            if step + 1 < levels:
-                gather_copy(r, half, step + 1).start()
+        buffer[r, place, floor] = joined.astype(BF16)
+        for copy in column_copies(r):
+            copy.start()
+
+    def spread(r):
+        for copy in column_copies(r):
+            copy.wait()
+        for copy in plane_copies(r):
+            copy.start()
 
     def collect(r):
-        relay(r, levels - 1)
-        for half in range(2):
-            block = buffer[r, half].reshape(members, ROWS // 2, HEAD_DIM).astype(F32)
-            for g in range(GROUPS // 2):
-                piece = block[:, g * Q_TOK : (g + 1) * Q_TOK, :]
-                feature = (half * GROUPS // 2 + g) * HEAD_DIM
-                rows[:, feature : feature + HEAD_DIM] = piece.reshape(
-                    members * Q_TOK, HEAD_DIM
-                ).astype(BF16)
+        for copy in plane_copies(r):
+            copy.wait()
+        for z in range(floors):
+            block = buffer[r, :, z].astype(F32)
+            for g in range(GROUPS):
+                piece = block[:, g * Q_TOK : (g + 1) * Q_TOK, :].reshape(plane * Q_TOK, HEAD_DIM)
+                rows[
+                    z * plane * Q_TOK : (z + 1) * plane * Q_TOK,
+                    g * HEAD_DIM : (g + 1) * HEAD_DIM,
+                ] = piece.astype(BF16)
 
     depth = GROUPS * HEAD_DIM
 
@@ -175,10 +184,10 @@
     limit = length[0] - base
 
     def one_round(r, _):
-        def hook(action):
-            @pl.when(r > 0)
+        def hook(action, back):
+            @pl.when(r >= back)
             def _():
-                action(r - 1)
+                action(r - back)
 
         lanes = [
             pl.ds(pl.multiple_of(head_of(r, i) * HEAD_DIM, HEAD_DIM), HEAD_DIM)
@@ -191,6 +200,7 @@
             stacked_rows(queries[:, pl.ds(pl.multiple_of(head_of(r, i) * depth, depth), depth)])
             for i in range(PAIR)
         ]
+        factors = [scales[pl.ds(head_of(r, i), 1), :] for i in range(PAIR)]
         tops = [jnp.full((ROWS, HEAD_DIM), NEG_FILL, F32) for _ in range(PAIR)]
         for c in range(own // CHUNK):
             span = slice(c * CHUNK, (c + 1) * CHUNK)
@@ -215,12 +225,10 @@
                 scores[i, :, span] = score
                 for v in range(CHUNK // HEAD_DIM):
                     tops[i] = jnp.maximum(tops[i], score[:, v * HEAD_DIM : (v + 1) * HEAD_DIM])
-            if c == 1:
-                hook(combine)
-            if c >= 3 and c % 2 == 1 and (c - 3) // 2 < levels - 2:
-                hook(lambda q, step=(c - 3) // 2: relay(q, step))
-        for step in range(min(levels - 2, (own // CHUNK - 2) // 2), levels - 1):
-            hook(lambda q, step=step: relay(q, step))
+            if c == 3:
+                hook(whole_product, 2)
+            if c == own // CHUNK - 2:
+                hook(combine, 1)
         for copy in codes_copies(r):
             copy.wait()
         for i in (1, 0):
@@ -243,22 +251,22 @@
                 product = jnp.dot(
                     weights.astype(BF16), codes[r, i, span, :], preferred_element_type=F32
                 )
-                part = part + product * scales[head_of(r, i), b]
+                part = part + product * factors[i][:, b : b + 1]
             total = jnp.sum(total, axis=1, keepdims=True)
             keep = mine if i == 0 else theirs
             keep[r, 0] = part
             keep[r, 1] = jnp.where(column < HALF, peak, total)
             if i == 1:
                 pair_copy(r).start()
-        hook(whole_product)
+        hook(spread, 1)
         return 0
 
     partial[...] = jnp.zeros_like(partial)
     lax.fori_loop(0, rounds, one_round, 0)
     final = rounds - 1
     combine(final)
-    for step in range(levels - 1):
-        relay(final, step)
+    whole_product(final - 1)
+    spread(final)
     collect(final)
     half_rows = members * Q_TOK // 2
     half_of = lambda n: pl.ds(pl.multiple_of(n * half_rows, half_rows), half_rows)
@@ -277,8 +285,8 @@
     own, rank = latents.shape[1:]
     cosine, sine = rope_tables(own * lax.axis_size("kv"))
     members = lax.axis_size("group")
-    levels = members.bit_length() - 1
-    assert members == 2**levels and lax.axis_size("kv") == 2
+    floors = 4 if members % 4 == 0 else 1
+    plane = members // floors
     depth, columns = out_weight.shape
     rounds = KV_HEADS // 2
     count = members * Q_TOK
@@ -290,7 +298,7 @@
     return pl.pallas_call(
         step_kernel,
         out_shape=jax.ShapeDtypeStruct((count // 2, columns), F32),
-        in_specs=[scalar, scalar] + [anywhere] * 4 + [near] * 4 + [anywhere],
+        in_specs=[scalar] + [anywhere] * 4 + [near] * 5 + [anywhere],
         out_specs=near,
         scratch_shapes=[
             pltpu.VMEM((rank, own), BF16),
@@ -298,11 +306,12 @@
             pltpu.VMEM((HALF, own), F32),
             pltpu.VMEM((HALF, own), F32),
             pltpu.VMEM((depth, columns), BF16),
+            pltpu.VMEM(scales.shape[:0:-1], F32),
             pltpu.VMEM((PAIR, ROWS, own), F32),
             pltpu.VMEM((rounds, 2, ROWS, HEAD_DIM), F32),
             pltpu.VMEM((rounds, 2, ROWS, HEAD_DIM), F32),
             pltpu.VMEM((rounds, 2, ROWS, HEAD_DIM), F32),
-            pltpu.VMEM((rounds, 2, *[2] * levels, ROWS // 2, HEAD_DIM), BF16),
+            pltpu.VMEM((rounds, plane, floors, ROWS, HEAD_DIM), BF16),
             pltpu.VMEM((count, GROUPS * HEAD_DIM), BF16),
             pltpu.VMEM((count, columns), F32),
             pltpu.VMEM((count // 2, columns), F32),
@@ -313,15 +322,17 @@
             dma((rounds,)),
             dma,
             dma,
-            dma((rounds, 2, levels)),
-            dma((rounds, 2, levels)),
+            dma((rounds, max(floors - 1, 1))),
+            dma((rounds, max(floors - 1, 1))),
+            dma((rounds, max(plane - 1, 1))),
+            dma((rounds, max(plane - 1, 1))),
         ],
         compiler_params=pltpu.CompilerParams(
-            collective_id=0, has_side_effects=True, vmem_limit_bytes=56 * 1024 * 1024
+            collective_id=0, has_side_effects=True, vmem_limit_bytes=54 * 1024 * 1024
         ),
         name="decode_step",
-    )(lengths, scales[0].astype(F32).T, latents[0].T, codes[0], jnp.asarray(cosine),
-      jnp.asarray(sine), queries[0], new_keys[0], new_values[0], key_factor, out_weight)
+    )(lengths, latents[0].T, codes[0], jnp.asarray(cosine), jnp.asarray(sine), scales[0].T,
+      queries[0], new_keys[0], new_values[0], key_factor, out_weight)
 
 
 def solution(mesh):

time: 69.3 us -> 50.3 us (0.73)
  Pallas kernels: 65.6 us -> 47.9 us
  other arithmetic: 1.28 us -> 0 us
    pallas_call x1, Pallas kernels: 65.6 us -> 47.9 us  [body(): pl.pallas_call(step_kernel, out_shape=jax.ShapeDtypeStruct((count // 2, c...]
    transpose x1 -> x0, other arithmetic: 1.28 us -> none  [body(): scales[0].astype(F32)]
where the time goes in v3:
time: 50.3 us; the launch traced here: 50.2 us
  Pallas kernels  47.9 us (95%)
  local copies, waits for them, and re-layouts  1.57 us (3%)
  between operations  0.66 us (1%)
    pallas_call x1, Pallas kernels, body(): pl.pallas_call(step_kernel, out_shape=jax.ShapeDtypeStruct((count // 2, c...  47.9 us
    unnamed x1, local copies, waits for them, and re-layouts  1.57 us

profile of v3, /device:TPU:0, one launch (start us, length us, event | category | flops | bytes accessed | tf_op | source)
XLA Modules:
  0.0 50.2 jit_solution(7049220355786655835)
XLA Ops:
  0.7 47.9 %decode_step.1 = f32[64,512]{1,0:T(8,128)} custom-call(s32[1]{0:T(128)S(6)} %copy.13.length, bf16[160,4096]{1,0:T(8,128)(2,1)} %bitcast.11, bf16[4096,1024]{1,0:T(8,128)(2,1)} %bitcast.10, f32[64,8192]{1,0:T(8,128)} %constant.4.clone.cosine_hbm, f32[64,8192]{1,0:T(8,128)} %constant.5.clone.sine_hbm, bf16[8,16]{1,0:T(8,128)(2,1)} %bitcast.15, ...), custom_call_target="tpu_custom_call" | custom-call | tf_op jit(solution)/shard_map/decode_step/pallas_call | solution.py:298
  48.6 1.6 %copy.14 = f32[64,512]{1,0:T(8,128)} copy(f32[64,512]{1,0:T(8,128)} %decode_step.1) | data formatting | bytes 262144

commit v4 on v3

--- a/solution.py
+++ b/solution.py
@@ -48,11 +48,12 @@
 
 
 def step_kernel(
-    length, latents_hbm, codes_hbm, cosine_hbm, sine_hbm, scales_in, queries, new_keys,
-    new_values, factor, weight_hbm, out,
+    length, latents_hbm, codes_hbm, cosine_hbm, sine_hbm, scales_hbm, queries_hbm,
+    new_keys_hbm, new_values_hbm, factor_hbm, weight_hbm, out,
+    scales_in, queries, late_keys, late_values, factor,
     latents, codes, cosine, sine, weight, scales, scores, mine, theirs, got, buffer, rows, partial,
     got_partial,
-    piece_sem, codes_sem, weight_sem, pair_send, pair_recv, last_send, last_recv,
+    small_sem, piece_sem, codes_sem, weight_sem, pair_send, pair_recv, last_send, last_recv,
     column_send, column_recv, plane_send, plane_recv,
 ):
     at = lax.axis_index("kv")
@@ -86,11 +87,27 @@
         for i in range(PAIR):
             lanes = pl.ds(pl.multiple_of(head_of(r, i) * HEAD_DIM, HEAD_DIM), HEAD_DIM)
             result.append(
-                pltpu.make_async_copy(codes_hbm.at[:, lanes], codes.at[r, i], codes_sem.at[r, i])
+                pltpu.make_async_copy(
+                    codes_hbm.at[:, lanes],
+                    codes.at[r, :, pl.ds(i * HEAD_DIM, HEAD_DIM)],
+                    codes_sem.at[r, i],
+                )
             )
         return result
 
     load = pltpu.make_async_copy(weight_hbm, weight, weight_sem)
+    small = [
+        pltpu.make_async_copy(source, target, small_sem.at[n])
+        for n, (source, target) in enumerate((
+            (factor_hbm, factor),
+            (queries_hbm, queries),
+            (new_keys_hbm, late_keys),
+            (new_values_hbm, late_values),
+            (scales_hbm, scales_in),
+        ))
+    ]
+    for copy in small:
+        copy.start()
     for n in range(pieces):
         for copy in piece_copies(n):
             copy.start()
@@ -104,6 +121,8 @@
     for peer in above + beside:
         pl.semaphore_signal(barrier, inc=1, device_id=(peer, at), device_id_type=MESH)
     pl.semaphore_wait(barrier, len(above) + len(beside) + 1)
+    for copy in small:
+        copy.wait()
     scales[...] = scales_in[...].astype(F32)
 
     def pair_copy(r):
@@ -225,40 +244,52 @@
                 scores[i, :, span] = score
                 for v in range(CHUNK // HEAD_DIM):
                     tops[i] = jnp.maximum(tops[i], score[:, v * HEAD_DIM : (v + 1) * HEAD_DIM])
-            if c == 3:
+            if c == 1:
+                hook(combine, 1)
+            if c == own // CHUNK - 3:
                 hook(whole_product, 2)
-            if c == own // CHUNK - 2:
-                hook(combine, 1)
+        hook(spread, 1)
         for copy in codes_copies(r):
             copy.wait()
-        for i in (1, 0):
+        peaks, totals, parts = [], [], []
+        for i in range(PAIR):
             fresh = lax.dot_general(
-                query[i], padded(new_keys[:, lanes[i]]), (((1,), (1,)), ((), ())),
+                query[i], padded(late_keys[:, lanes[i]]), (((1,), (1,)), ((), ())),
                 preferred_element_type=F32,
             )
             fresh = jnp.where(causal, fresh, NEG_FILL)
             peak = jnp.max(jnp.maximum(tops[i], fresh), axis=1, keepdims=True) * TO_EXP2
+            peaks.append(jnp.broadcast_to(peak, (ROWS, BLK)))
             weights = jnp.where(causal, jnp.exp2(fresh * TO_EXP2 - peak), 0.0)
-            total = weights
-            part = jnp.dot(
-                weights.astype(BF16), padded(new_values[:, lanes[i]]), preferred_element_type=F32
-            )
-            for b in range(own // BLK):
-                span = slice(b * BLK, (b + 1) * BLK)
-                weights = jnp.exp2(scores[i, :, span] * TO_EXP2 - peak)
+            totals.append(weights)
+            parts.append(
+                jnp.dot(
+                    weights.astype(BF16), padded(late_values[:, lanes[i]]),
+                    preferred_element_type=F32,
+                )
+            )
+        for b in range(own // BLK):
+            span = slice(b * BLK, (b + 1) * BLK)
+            both = []
+            for i in range(PAIR):
+                weights = jnp.exp2(scores[i, :, span] * TO_EXP2 - peaks[i])
                 for v in range(BLK // HEAD_DIM):
-                    total = total + weights[:, v * HEAD_DIM : (v + 1) * HEAD_DIM]
-                product = jnp.dot(
-                    weights.astype(BF16), codes[r, i, span, :], preferred_element_type=F32
-                )
-                part = part + product * factors[i][:, b : b + 1]
-            total = jnp.sum(total, axis=1, keepdims=True)
-            keep = mine if i == 0 else theirs
-            keep[r, 0] = part
-            keep[r, 1] = jnp.where(column < HALF, peak, total)
+                    totals[i] = totals[i] + weights[:, v * HEAD_DIM : (v + 1) * HEAD_DIM]
+                both.append(weights.astype(BF16))
+            product = jnp.dot(
+                jnp.concatenate(both, axis=0), codes[r, span, :], preferred_element_type=F32
+            )
+            for i in range(PAIR):
+                own_part = product[
+                    i * ROWS : (i + 1) * ROWS, i * HEAD_DIM : (i + 1) * HEAD_DIM
+                ]
+                parts[i] = parts[i] + own_part * factors[i][:, b : b + 1]
+        for i, keep in ((1, theirs), (0, mine)):
+            total = jnp.sum(totals[i], axis=1, keepdims=True)
+            keep[r, 0] = parts[i]
+            keep[r, 1] = jnp.where(column < HALF, peaks[i][:, :HEAD_DIM], total)
             if i == 1:
                 pair_copy(r).start()
-        hook(spread, 1)
         return 0
 
     partial[...] = jnp.zeros_like(partial)
@@ -298,11 +329,16 @@
     return pl.pallas_call(
         step_kernel,
         out_shape=jax.ShapeDtypeStruct((count // 2, columns), F32),
-        in_specs=[scalar] + [anywhere] * 4 + [near] * 5 + [anywhere],
+        in_specs=[scalar] + [anywhere] * 10,
         out_specs=near,
         scratch_shapes=[
+            pltpu.VMEM(scales.shape[:0:-1], BF16),
+            pltpu.VMEM(queries.shape[1:], BF16),
+            pltpu.VMEM(new_keys.shape[1:], BF16),
+            pltpu.VMEM(new_values.shape[1:], BF16),
+            pltpu.VMEM(key_factor.shape, BF16),
             pltpu.VMEM((rank, own), BF16),
-            pltpu.VMEM((rounds, PAIR, own, HEAD_DIM), BF16),
+            pltpu.VMEM((rounds, own, PAIR * HEAD_DIM), BF16),
             pltpu.VMEM((HALF, own), F32),
             pltpu.VMEM((HALF, own), F32),
             pltpu.VMEM((depth, columns), BF16),
@@ -315,6 +351,7 @@
             pltpu.VMEM((count, GROUPS * HEAD_DIM), BF16),
             pltpu.VMEM((count, columns), F32),
             pltpu.VMEM((count // 2, columns), F32),
+            dma((5,)),
             dma((3, pieces)),
             dma((rounds, PAIR)),
             dma,
@@ -328,7 +365,7 @@
             dma((rounds, max(plane - 1, 1))),
         ],
         compiler_params=pltpu.CompilerParams(
-            collective_id=0, has_side_effects=True, vmem_limit_bytes=54 * 1024 * 1024
+            collective_id=0, has_side_effects=True, vmem_limit_bytes=107 * 512 * 1024
         ),
         name="decode_step",
     )(lengths, latents[0].T, codes[0], jnp.asarray(cosine), jnp.asarray(sine), scales[0].T,

time: 50.3 us -> 43.6 us (0.87)
  Pallas kernels: 47.9 us -> 38.9 us
  local copies, waits for them, and re-layouts: 1.57 us -> 3.67 us
    pallas_call x1, Pallas kernels: 47.9 us -> 38.9 us  [body(): pl.pallas_call(step_kernel, out_shape=jax.ShapeDtypeStruct((count // 2, c...]
    unnamed x1 -> x9, local copies, waits for them, and re-layouts: 1.57 us -> 3.67 us
where the time goes in v4:
time: 43.6 us; the launch traced here: 43.2 us
  Pallas kernels  38.9 us (89%)
  local copies, waits for them, and re-layouts  3.67 us (8%)
  between operations  0.67 us (2%)
    pallas_call x1, Pallas kernels, body(): pl.pallas_call(step_kernel, out_shape=jax.ShapeDtypeStruct((count // 2, c...  38.9 us
    unnamed x9, local copies, waits for them, and re-layouts  3.67 us

profile of v4, /device:TPU:0, one launch (start us, length us, event | category | flops | bytes accessed | tf_op | source)
XLA Modules:
  0.0 43.2 jit_solution(303251541190142319)
XLA Ops:
  0.7 0.0 copy-start
  0.7 0.9 %copy-done = bf16[1,8,8192]{2,1,0:T(8,128)(2,1)S(1)} copy-done((bf16[1,8,8192]{2,1,0:T(8,128)(2,1)S(1)}, bf16[1,8,8192]{2,1,0:T(8,128)(2,1)}, u32[]{:S(2)}) %copy-start) | copy-done | bytes 131096
  1.6 0.0 copy-start.1
  1.6 0.7 %copy-done.1 = bf16[1,8,1024]{2,1,0:T(8,128)(2,1)S(1)} copy-done((bf16[1,8,1024]{2,1,0:T(8,128)(2,1)S(1)}, bf16[1,8,1024]{2,1,0:T(8,128)(2,1)}, u32[]{:S(2)}) %copy-start.1) | copy-done | bytes 16408
  2.3 0.0 copy-start.2
  2.3 0.7 %copy-done.2 = bf16[1,8,1024]{2,1,0:T(8,128)(2,1)S(1)} copy-done((bf16[1,8,1024]{2,1,0:T(8,128)(2,1)S(1)}, bf16[1,8,1024]{2,1,0:T(8,128)(2,1)}, u32[]{:S(2)}) %copy-start.2) | copy-done | bytes 16408
  3.0 0.0 copy-start.3
  3.0 0.7 %copy-done.3 = bf16[1,16,8]{1,2,0:T(8,128)(2,1)S(1)} copy-done((bf16[1,16,8]{1,2,0:T(8,128)(2,1)S(1)}, bf16[1,16,8]{1,2,0:T(8,128)(2,1)}, u32[]{:S(2)}) %copy-start.3) | copy-done | bytes 280
  3.7 38.9 %decode_step.1 = f32[64,512]{1,0:T(8,128)S(1)} custom-call(s32[1]{0:T(128)S(6)} %copy.13.length, bf16[160,4096]{1,0:T(8,128)(2,1)} %bitcast.15, bf16[4096,1024]{1,0:T(8,128)(2,1)} %bitcast.14, f32[64,8192]{1,0:T(8,128)} %constant.4.clone.cosine_hbm, f32[64,8192]{1,0:T(8,128)} %constant.5.clone.sine_hbm, bf16[8,16]{1,0:T(8,128)(2,1)S(1)} %bitcast.13, ...), custom_call_target="tpu_custom_call" | custom-call | tf_op jit(solution)/shard_map/decode_step/pallas_call | solution.py:329
  42.5 0.7 %copy.14 = f32[64,512]{1,0:T(8,128)} copy(f32[64,512]{1,0:T(8,128)S(1)} %decode_step.1) | data formatting | bytes 262144
Async XLA Ops:
  0.7 0.9 %copy-start = (bf16[1,8,8192]{2,1,0:T(8,128)(2,1)S(1)}, bf16[1,8,8192]{2,1,0:T(8,128)(2,1)}, u32[]{:S(2)}) copy-start(bf16[1,8,8192]{2,1,0:T(8,128)(2,1)} %param.15) | copy-start | bytes 393220
  1.6 0.7 %copy-start.1 = (bf16[1,8,1024]{2,1,0:T(8,128)(2,1)S(1)}, bf16[1,8,1024]{2,1,0:T(8,128)(2,1)}, u32[]{:S(2)}) copy-start(bf16[1,8,1024]{2,1,0:T(8,128)(2,1)} %param.16) | copy-start | bytes 49156
  2.3 0.7 %copy-start.2 = (bf16[1,8,1024]{2,1,0:T(8,128)(2,1)S(1)}, bf16[1,8,1024]{2,1,0:T(8,128)(2,1)}, u32[]{:S(2)}) copy-start(bf16[1,8,1024]{2,1,0:T(8,128)(2,1)} %param.17) | copy-start | bytes 49156
  3.0 0.7 %copy-start.3 = (bf16[1,16,8]{1,2,0:T(8,128)(2,1)S(1)}, bf16[1,16,8]{1,2,0:T(8,128)(2,1)}, u32[]{:S(2)}) copy-start(bf16[1,16,8]{1,2,0:T(8,128)(2,1)} %param.14) | copy-start | bytes 772

commit v5 on v4

--- a/solution.py
+++ b/solution.py
@@ -245,10 +245,10 @@
                 for v in range(CHUNK // HEAD_DIM):
                     tops[i] = jnp.maximum(tops[i], score[:, v * HEAD_DIM : (v + 1) * HEAD_DIM])
             if c == 1:
-                hook(combine, 1)
-            if c == own // CHUNK - 3:
-                hook(whole_product, 2)
-        hook(spread, 1)
+                hook(whole_product, 3)
+            if c == 3:
+                hook(spread, 2)
+        hook(combine, 1)
         for copy in codes_copies(r):
             copy.wait()
         peaks, totals, parts = [], [], []
@@ -296,8 +296,10 @@
     lax.fori_loop(0, rounds, one_round, 0)
     final = rounds - 1
     combine(final)
+    spread(final - 1)
+    whole_product(final - 2)
+    spread(final)
     whole_product(final - 1)
-    spread(final)
     collect(final)
     half_rows = members * Q_TOK // 2
     half_of = lambda n: pl.ds(pl.multiple_of(n * half_rows, half_rows), half_rows)
@@ -365,7 +367,7 @@
             dma((rounds, max(plane - 1, 1))),
         ],
         compiler_params=pltpu.CompilerParams(
-            collective_id=0, has_side_effects=True, vmem_limit_bytes=107 * 512 * 1024
+            collective_id=0, has_side_effects=True, vmem_limit_bytes=54 * 1024 * 1024
         ),
         name="decode_step",
     )(lengths, latents[0].T, codes[0], jnp.asarray(cosine), jnp.asarray(sine), scales[0].T,

time: 43.6 us -> 40.5 us (0.929)
  local copies, waits for them, and re-layouts: 3.67 us -> 1.57 us
  Pallas kernels: 38.9 us -> 38.1 us
    unnamed x9 -> x1, local copies, waits for them, and re-layouts: 3.67 us -> 1.57 us
    pallas_call x1, Pallas kernels: 38.9 us -> 38.1 us  [body(): pl.pallas_call(step_kernel, out_shape=jax.ShapeDtypeStruct((count // 2, c...]
where the time goes in v5:
time: 40.5 us; the launch traced here: 40.3 us
  Pallas kernels  38.1 us (94%)
  local copies, waits for them, and re-layouts  1.57 us (4%)
  between operations  0.66 us (2%)
    pallas_call x1, Pallas kernels, body(): pl.pallas_call(step_kernel, out_shape=jax.ShapeDtypeStruct((count // 2, c...  38.1 us
    unnamed x1, local copies, waits for them, and re-layouts  1.57 us

profile of v5, /device:TPU:0, one launch (start us, length us, event | category | flops | bytes accessed | tf_op | source)
XLA Modules:
  0.0 40.3 jit_solution(7253507038163381768)
XLA Ops:
  0.7 38.1 %decode_step.1 = f32[64,512]{1,0:T(8,128)} custom-call(s32[1]{0:T(128)S(6)} %copy.13.length, bf16[160,4096]{1,0:T(8,128)(2,1)} %bitcast.11, bf16[4096,1024]{1,0:T(8,128)(2,1)} %bitcast.10, f32[64,8192]{1,0:T(8,128)} %constant.4.clone.cosine_hbm, f32[64,8192]{1,0:T(8,128)} %constant.5.clone.sine_hbm, bf16[8,16]{1,0:T(8,128)(2,1)} %bitcast.15, ...), custom_call_target="tpu_custom_call" | custom-call | tf_op jit(solution)/shard_map/decode_step/pallas_call | solution.py:331
  38.8 1.6 %copy.14 = f32[64,512]{1,0:T(8,128)} copy(f32[64,512]{1,0:T(8,128)} %decode_step.1) | data formatting | bytes 262144

commit v6 on v5

--- a/solution.py
+++ b/solution.py
@@ -51,7 +51,7 @@
     length, latents_hbm, codes_hbm, cosine_hbm, sine_hbm, scales_hbm, queries_hbm,
     new_keys_hbm, new_values_hbm, factor_hbm, weight_hbm, out,
     scales_in, queries, late_keys, late_values, factor,
-    latents, codes, cosine, sine, weight, scales, scores, mine, theirs, got, buffer, rows, partial,
+    latents, codes, cosine, sine, weight, scales, scores, state, mine, theirs, got, buffer, rows, partial,
     got_partial,
     small_sem, piece_sem, codes_sem, weight_sem, pair_send, pair_recv, last_send, last_recv,
     column_send, column_recv, plane_send, plane_recv,
@@ -111,10 +111,8 @@
     for n in range(pieces):
         for copy in piece_copies(n):
             copy.start()
-    for r in range(rounds):
-        for copy in codes_copies(r):
-            copy.start()
-    load.start()
+    for copy in codes_copies(0):
+        copy.start()
 
     barrier = pltpu.get_barrier_semaphore()
     pl.semaphore_signal(barrier, inc=1, device_id=(me, other), device_id_type=MESH)
@@ -202,98 +200,129 @@
     causal = jnp.logical_and(column <= token, at == 0)
     limit = length[0] - base
 
+    def lanes_of(r, i):
+        return pl.ds(pl.multiple_of(head_of(r, i) * HEAD_DIM, HEAD_DIM), HEAD_DIM)
+
+    def prepare(r):
+        turned = jnp.concatenate(
+            [factor[:, lanes_of(r, i)].astype(F32).T for i in range(PAIR)], axis=0
+        ).astype(BF16)
+        query = [
+            stacked_rows(queries[:, pl.ds(pl.multiple_of(head_of(r, i) * depth, depth), depth)])
+            for i in range(PAIR)
+        ]
+        tops = [jnp.full((ROWS, HEAD_DIM), NEG_FILL, F32) for _ in range(PAIR)]
+        return turned, query, tops
+
+    def score_chunk(slot, c, turned, query, tops):
+        span = slice(c * CHUNK, (c + 1) * CHUNK)
+        keys = jnp.dot(turned, latents[:, span], preferred_element_type=F32)
+        cos, sin = cosine[:, span], sine[:, span]
+        valid = c * CHUNK + lax.broadcasted_iota(jnp.int32, (1, CHUNK), 1) < limit
+        for i in range(PAIR):
+            low = keys[i * HEAD_DIM : i * HEAD_DIM + HALF]
+            high = keys[i * HEAD_DIM + HALF : (i + 1) * HEAD_DIM]
+            rotated = jnp.concatenate(
+                [low * cos - high * sin, high * cos + low * sin], axis=0
+            ).astype(BF16)
+            score = jnp.dot(query[i], rotated, preferred_element_type=F32)
+            score = jnp.where(valid, score, NEG_FILL)
+            scores[slot, i, :, span] = score
+            for v in range(CHUNK // HEAD_DIM):
+                tops[i] = jnp.maximum(tops[i], score[:, v * HEAD_DIM : (v + 1) * HEAD_DIM])
+
+    def close_scores(r, query, tops):
+        for i in range(PAIR):
+            fresh = lax.dot_general(
+                query[i], padded(late_keys[:, lanes_of(r, i)]), (((1,), (1,)), ((), ())),
+                preferred_element_type=F32,
+            )
+            fresh = jnp.where(causal, fresh, NEG_FILL)
+            peak = jnp.max(jnp.maximum(tops[i], fresh), axis=1, keepdims=True) * TO_EXP2
+            weights = jnp.where(causal, jnp.exp2(fresh * TO_EXP2 - peak), 0.0)
+            state[0, i] = jnp.broadcast_to(peak, (ROWS, HEAD_DIM))
+            state[1, i] = weights
+            state[2, i] = jnp.dot(
+                weights.astype(BF16), padded(late_values[:, lanes_of(r, i)]),
+                preferred_element_type=F32,
+            )
+
+    def open_values(r):
+        factors = [scales[pl.ds(head_of(r, i), 1), :] for i in range(PAIR)]
+        peaks = [state[0, i] for i in range(PAIR)]
+        return factors, peaks, [state[1, i] for i in range(PAIR)], [state[2, i] for i in range(PAIR)]
+
+    def value_block(r, slot, b, factors, peaks, totals, parts):
+        span = slice(b * BLK, (b + 1) * BLK)
+        both = []
+        for i in range(PAIR):
+            peak = jnp.concatenate([peaks[i]] * (BLK // HEAD_DIM), axis=1)
+            weights = jnp.exp2(scores[slot, i, :, span] * TO_EXP2 - peak)
+            for v in range(BLK // HEAD_DIM):
+                totals[i] = totals[i] + weights[:, v * HEAD_DIM : (v + 1) * HEAD_DIM]
+            both.append(weights.astype(BF16))
+        product = jnp.dot(
+            jnp.concatenate(both, axis=0), codes[r, span, :], preferred_element_type=F32
+        )
+        for i in range(PAIR):
+            own_part = product[i * ROWS : (i + 1) * ROWS, i * HEAD_DIM : (i + 1) * HEAD_DIM]
+            parts[i] = parts[i] + own_part * factors[i][:, b : b + 1]
+
+    def close_values(r, factors, peaks, totals, parts):
+        for i, keep in ((1, theirs), (0, mine)):
+            total = jnp.sum(totals[i], axis=1, keepdims=True)
+            keep[r, 0] = parts[i]
+            keep[r, 1] = jnp.where(column < HALF, peaks[i], total)
+        pair_copy(r).start()
+
+    chunks = own // CHUNK
+    blocks = CHUNK // BLK
+
     def one_round(r, _):
         def hook(action, back):
             @pl.when(r >= back)
             def _():
                 action(r - back)
 
-        lanes = [
-            pl.ds(pl.multiple_of(head_of(r, i) * HEAD_DIM, HEAD_DIM), HEAD_DIM)
-            for i in range(PAIR)
-        ]
-        turned = jnp.concatenate(
-            [factor[:, lanes[i]].astype(F32).T for i in range(PAIR)], axis=0
-        ).astype(BF16)
-        query = [
-            stacked_rows(queries[:, pl.ds(pl.multiple_of(head_of(r, i) * depth, depth), depth)])
-            for i in range(PAIR)
-        ]
-        factors = [scales[pl.ds(head_of(r, i), 1), :] for i in range(PAIR)]
-        tops = [jnp.full((ROWS, HEAD_DIM), NEG_FILL, F32) for _ in range(PAIR)]
-        for c in range(own // CHUNK):
-            span = slice(c * CHUNK, (c + 1) * CHUNK)
-            if c * CHUNK % wide == 0:
-
-                @pl.when(r == 0)
-                def _(n=c * CHUNK // wide):
-                    for copy in piece_copies(n):
-                        copy.wait()
-
-            keys = jnp.dot(turned, latents[:, span], preferred_element_type=F32)
-            cos, sin = cosine[:, span], sine[:, span]
-            valid = c * CHUNK + lax.broadcasted_iota(jnp.int32, (1, CHUNK), 1) < limit
-            for i in range(PAIR):
-                low = keys[i * HEAD_DIM : i * HEAD_DIM + HALF]
-                high = keys[i * HEAD_DIM + HALF : (i + 1) * HEAD_DIM]
-                rotated = jnp.concatenate(
-                    [low * cos - high * sin, high * cos + low * sin], axis=0
-                ).astype(BF16)
-                score = jnp.dot(query[i], rotated, preferred_element_type=F32)
-                score = jnp.where(valid, score, NEG_FILL)
-                scores[i, :, span] = score
-                for v in range(CHUNK // HEAD_DIM):
-                    tops[i] = jnp.maximum(tops[i], score[:, v * HEAD_DIM : (v + 1) * HEAD_DIM])
-            if c == 1:
+        slot, before = r % 2, (r + 1) % 2
+        for copy in codes_copies(r):
+            copy.start()
+        for copy in codes_copies(r - 1):
+            copy.wait()
+        ready = prepare(r)
+        held = open_values(r - 1)
+        for c in range(chunks):
+            score_chunk(slot, c, *ready)
+            for b in range(c * blocks, (c + 1) * blocks):
+                value_block(r - 1, before, b, *held)
+            if c == 3:
+                hook(combine, 2)
+            if c == 5:
                 hook(whole_product, 3)
-            if c == 3:
-                hook(spread, 2)
-        hook(combine, 1)
-        for copy in codes_copies(r):
-            copy.wait()
-        peaks, totals, parts = [], [], []
-        for i in range(PAIR):
-            fresh = lax.dot_general(
-                query[i], padded(late_keys[:, lanes[i]]), (((1,), (1,)), ((), ())),
-                preferred_element_type=F32,
-            )
-            fresh = jnp.where(causal, fresh, NEG_FILL)
-            peak = jnp.max(jnp.maximum(tops[i], fresh), axis=1, keepdims=True) * TO_EXP2
-            peaks.append(jnp.broadcast_to(peak, (ROWS, BLK)))
-            weights = jnp.where(causal, jnp.exp2(fresh * TO_EXP2 - peak), 0.0)
-            totals.append(weights)
-            parts.append(
-                jnp.dot(
-                    weights.astype(BF16), padded(late_values[:, lanes[i]]),
-                    preferred_element_type=F32,
-                )
-            )
-        for b in range(own // BLK):
-            span = slice(b * BLK, (b + 1) * BLK)
-            both = []
-            for i in range(PAIR):
-                weights = jnp.exp2(scores[i, :, span] * TO_EXP2 - peaks[i])
-                for v in range(BLK // HEAD_DIM):
-                    totals[i] = totals[i] + weights[:, v * HEAD_DIM : (v + 1) * HEAD_DIM]
-                both.append(weights.astype(BF16))
-            product = jnp.dot(
-                jnp.concatenate(both, axis=0), codes[r, span, :], preferred_element_type=F32
-            )
-            for i in range(PAIR):
-                own_part = product[
-                    i * ROWS : (i + 1) * ROWS, i * HEAD_DIM : (i + 1) * HEAD_DIM
-                ]
-                parts[i] = parts[i] + own_part * factors[i][:, b : b + 1]
-        for i, keep in ((1, theirs), (0, mine)):
-            total = jnp.sum(totals[i], axis=1, keepdims=True)
-            keep[r, 0] = parts[i]
-            keep[r, 1] = jnp.where(column < HALF, peaks[i][:, :HEAD_DIM], total)
-            if i == 1:
-                pair_copy(r).start()
+        close_values(r - 1, *held)
+        close_scores(r, ready[1], ready[2])
+        hook(spread, 2)
         return 0
 
     partial[...] = jnp.zeros_like(partial)
-    lax.fori_loop(0, rounds, one_round, 0)
+    ready = prepare(0)
+    for c in range(chunks):
+        if c * CHUNK % wide == 0:
+            for copy in piece_copies(c * CHUNK // wide):
+                copy.wait()
+        score_chunk(0, c, *ready)
+    close_scores(0, ready[1], ready[2])
+    load.start()
+    lax.fori_loop(1, rounds, one_round, 0)
+    last_round = rounds - 1
+    for copy in codes_copies(last_round):
+        copy.wait()
+    held = open_values(last_round)
+    for b in range(chunks * blocks):
+        value_block(last_round, last_round % 2, b, *held)
+        if b == chunks * blocks * 3 // 4 - 1:
+            combine(last_round - 1)
+    close_values(last_round, *held)
     final = rounds - 1
     combine(final)
     spread(final - 1)
@@ -345,7 +374,8 @@
             pltpu.VMEM((HALF, own), F32),
             pltpu.VMEM((depth, columns), BF16),
             pltpu.VMEM(scales.shape[:0:-1], F32),
-            pltpu.VMEM((PAIR, ROWS, own), F32),
+            pltpu.VMEM((2, PAIR, ROWS, own), F32),
+            pltpu.VMEM((3, PAIR, ROWS, HEAD_DIM), F32),
             pltpu.VMEM((rounds, 2, ROWS, HEAD_DIM), F32),
             pltpu.VMEM((rounds, 2, ROWS, HEAD_DIM), F32),
             pltpu.VMEM((rounds, 2, ROWS, HEAD_DIM), F32),

time: 40.5 us -> 41.9 us (1.035)
  Pallas kernels: 38.1 us -> 39.5 us
    pallas_call x1, Pallas kernels: 38.1 us -> 39.5 us  [body(): pl.pallas_call(step_kernel, out_shape=jax.ShapeDtypeStruct((count // 2, c...]
where the time goes in v6:
time: 41.9 us; the launch traced here: 41.7 us
  Pallas kernels  39.5 us (94%)
  local copies, waits for them, and re-layouts  1.57 us (4%)
  between operations  0.66 us (2%)
    pallas_call x1, Pallas kernels, body(): pl.pallas_call(step_kernel, out_shape=jax.ShapeDtypeStruct((count // 2, c...  39.5 us
    unnamed x1, local copies, waits for them, and re-layouts  1.57 us

profile of v6, /device:TPU:0, one launch (start us, length us, event | category | flops | bytes accessed | tf_op | source)
XLA Modules:
  0.0 41.7 jit_solution(13496959298509888267)
XLA Ops:
  0.7 39.5 %decode_step.1 = f32[64,512]{1,0:T(8,128)} custom-call(s32[1]{0:T(128)S(6)} %copy.13.length, bf16[160,4096]{1,0:T(8,128)(2,1)} %bitcast.11, bf16[4096,1024]{1,0:T(8,128)(2,1)} %bitcast.10, f32[64,8192]{1,0:T(8,128)} %constant.4.clone.cosine_hbm, f32[64,8192]{1,0:T(8,128)} %constant.5.clone.sine_hbm, bf16[8,16]{1,0:T(8,128)(2,1)} %bitcast.15, ...), custom_call_target="tpu_custom_call" | custom-call | tf_op jit(solution)/shard_map/decode_step/pallas_call | solution.py:360
  40.1 1.6 %copy.14 = f32[64,512]{1,0:T(8,128)} copy(f32[64,512]{1,0:T(8,128)} %decode_step.1) | data formatting | bytes 262144

commit v7 on v5

--- a/solution.py
+++ b/solution.py
@@ -17,7 +17,7 @@
 Q_TOK = 8
 ROWS = Q_TOK * GROUPS
 PAIR = 2
-CHUNK = 512
+CHUNK = 256
 ROPE_BASE = 500000.0
 NEG_FILL = -1e30
 TO_EXP2 = math.log2(math.e) / math.sqrt(HEAD_DIM)
@@ -111,10 +111,8 @@
     for n in range(pieces):
         for copy in piece_copies(n):
             copy.start()
-    for r in range(rounds):
-        for copy in codes_copies(r):
-            copy.start()
-    load.start()
+    for copy in codes_copies(0):
+        copy.start()
 
     barrier = pltpu.get_barrier_semaphore()
     pl.semaphore_signal(barrier, inc=1, device_id=(me, other), device_id_type=MESH)
@@ -244,11 +242,20 @@
                 scores[i, :, span] = score
                 for v in range(CHUNK // HEAD_DIM):
                     tops[i] = jnp.maximum(tops[i], score[:, v * HEAD_DIM : (v + 1) * HEAD_DIM])
-            if c == 1:
+            if c == 3:
                 hook(whole_product, 3)
-            if c == 3:
+            if c == 7:
                 hook(spread, 2)
         hook(combine, 1)
+        @pl.when(r == 0)
+        def _():
+            load.start()
+
+        @pl.when(r + 1 < rounds)
+        def _():
+            for copy in codes_copies(r + 1):
+                copy.start()
+
         for copy in codes_copies(r):
             copy.wait()
         peaks, totals, parts = [], [], []

time: 40.5 us -> 41.6 us (1.027)
  Pallas kernels: 38.1 us -> 39.2 us
    pallas_call x1, Pallas kernels: 38.1 us -> 39.2 us  [body(): pl.pallas_call(step_kernel, out_shape=jax.ShapeDtypeStruct((count // 2, c...]
where the time goes in v7:
time: 41.6 us; the launch traced here: 41.4 us
  Pallas kernels  39.2 us (94%)
  local copies, waits for them, and re-layouts  1.57 us (4%)
  between operations  0.66 us (2%)
    pallas_call x1, Pallas kernels, body(): pl.pallas_call(step_kernel, out_shape=jax.ShapeDtypeStruct((count // 2, c...  39.2 us
    unnamed x1, local copies, waits for them, and re-layouts  1.57 us

profile of v7, /device:TPU:0, one launch (start us, length us, event | category | flops | bytes accessed | tf_op | source)
XLA Modules:
  0.0 41.4 jit_solution(3827737369556896030)
XLA Ops:
  0.7 39.2 %decode_step.1 = f32[64,512]{1,0:T(8,128)} custom-call(s32[1]{0:T(128)S(6)} %copy.13.length, bf16[160,4096]{1,0:T(8,128)(2,1)} %bitcast.11, bf16[4096,1024]{1,0:T(8,128)(2,1)} %bitcast.10, f32[64,8192]{1,0:T(8,128)} %constant.4.clone.cosine_hbm, f32[64,8192]{1,0:T(8,128)} %constant.5.clone.sine_hbm, bf16[8,16]{1,0:T(8,128)(2,1)} %bitcast.15, ...), custom_call_target="tpu_custom_call" | custom-call | tf_op jit(solution)/shard_map/decode_step/pallas_call | solution.py:338
  39.8 1.6 %copy.14 = f32[64,512]{1,0:T(8,128)} copy(f32[64,512]{1,0:T(8,128)} %decode_step.1) | data formatting | bytes 262144
